TPU v7x, 32 devices: a whole 2x2x4 slice. The times are simulated.
32 devices in a mesh: seq: 2 (over x), tm: 16 (over z, y, core).
Axes of the slice: x: 2, y: 2, z: 4, core: 2. Of those that a mesh axis runs over, the one named last changes fastest.
Arguments:
- layer_input: bfloat16 [2, 4096, 1024], P('seq', 'tm'), may hold values from -6 to 6
- routes: int32 [2, 4096, 8, 2], P('seq', 'tm'), may hold values from 0 to 4, all different within a row
- memory_lengths: int32 [2, 16], P('seq', 'tm'), may hold values from 0 to 256, as said below
- norm_gains: bfloat16 [2, 1024], replicated, may hold values from 0.5 to 1.5
- w_query: bfloat16 [1024, 448], replicated, may hold values from -0.25 to 0.25
- w_key: bfloat16 [1024, 448], replicated, may hold values from -0.25 to 0.25
- w_value: bfloat16 [1024, 2240], replicated, may hold values from -0.1875 to 0.1875
- w_router: bfloat16 [1024, 40], replicated, may hold values from -0.125 to 0.125
- w_output: bfloat16 [2240, 1024], replicated, may hold values from -3.5 to 3.5
- w_up: bfloat16 [1024, 4096], replicated, may hold values from -0.1875 to 0.1875
- w_down: bfloat16 [4096, 1024], replicated, may hold values from -0.09375 to 0.09375
- output_cot: bfloat16 [2, 4096, 1024], P('seq', 'tm'), may hold values from -6 to 6
Outputs:
- layer_output: bfloat16 [2, 4096, 1024], P('seq', 'tm')
- input_grad: float32 [2, 4096, 1024], P('seq', 'tm')
- gains_grad: float32 [2, 1024], P(None, ('seq', 'tm'))
- query_weight_grad: float32 [1024, 448], P(('seq', 'tm'))
- key_weight_grad: float32 [1024, 448], P(('seq', 'tm'))
- value_weight_grad: float32 [1024, 2240], P(('seq', 'tm'))
- router_weight_grad: float32 [1024, 40], P(('seq', 'tm'))
- output_weight_grad: float32 [2240, 1024], P(None, ('seq', 'tm'))
- up_weight_grad: float32 [1024, 4096], P(('seq', 'tm'))
- down_weight_grad: float32 [4096, 1024], P(None, ('seq', 'tm'))
Inputs may be any that keep to these rules, and one draw needn't show every extreme that they name: `routes`: each token names two different experts for each head's value branch and output branch. `memory_lengths`: the first segment of each sequence has 0; each sequence has a segment with exactly 256; all other segments have 1 to 256.
All inputs are finite; a program needn't handle non-finite values.
Results may differ from a plain program's by a relative error of at most 0.012.
The roundings to bfloat16 on the way count: a program that leaves them out, or rounds other values in their place, can miss the bound.
Values may be sent and summed in bfloat16 or wider, within the bound.
A program may use at most 256 MiB of HBM per device.

v0:
```python
import jax
import jax.numpy as jnp
from jax import lax
from jax.sharding import PartitionSpec as P

H = 4
DH = 112
E = 5


epsilon = 1e-05


def passed_along(value, axis, steps):
    count = lax.axis_size(axis)
    initial, last = (max(0, -steps), min(count, count - steps))
    return lax.ppermute(value, axis, [(source, source + steps) for source in range(initial, last)])


def normalize(values, gain_vec):
    centre = values - jnp.mean(values, axis=-1, keepdims=True)
    spread = jnp.mean(centre * centre, axis=-1, keepdims=True)
    return centre * lax.rsqrt(spread + epsilon) * gain_vec


def exact_gelu(arg_in):
    return jax.nn.gelu(arg_in, approximate=False)


def matmul(left_op, right_op):
    return jnp.dot(left_op, right_op, preferred_element_type=jnp.float32)


def times_tr(left_op, right_op):
    return lax.dot_general(
        left_op, right_op, (((1,), (1,)), ((), ())), preferred_element_type=jnp.float32
    )


def tr_times(left_op, right_op):
    return lax.dot_general(
        left_op, right_op, (((0,), (0,)), ((), ())), preferred_element_type=jnp.float32
    )


def one_hot_routes(route_ids):
    return jnp.sum(
        (route_ids[..., None] == jnp.arange(E, dtype=jnp.int32)).astype(jnp.float32), axis=-2
    )


def attention_mask(memory_length, seg_len):
    query_pos = jnp.arange(seg_len, dtype=jnp.int32)[:, None]
    key_pos = jnp.arange(2 * seg_len, dtype=jnp.int32)[None, :]
    return jnp.where(
        key_pos < seg_len, key_pos >= seg_len - memory_length, key_pos - seg_len <= query_pos
    )


def per_device(
    layer_input,
    routes,
    memory_lengths,
    norm_gains,
    w_query,
    w_key,
    w_value,
    w_router,
    w_output,
    w_up,
    w_down,
    output_cot,
):
    seg_len = layer_input.shape[1]
    own_rows = layer_input[0].astype(jnp.float32)
    memory_length = memory_lengths[0, 0]
    gains_f = norm_gains.astype(jnp.float32)
    first_gain = gains_f[0]
    second_gain = gains_f[1]
    scale_factor = DH ** (-0.5)
    allowed = attention_mask(memory_length, seg_len)
    onehot = one_hot_routes(routes[0])
    unit_normed = normalize(own_rows, jnp.ones_like(first_gain))
    own_normed = (unit_normed * first_gain).astype(jnp.bfloat16)

    def projections():
        queries = matmul(own_normed, w_query).astype(jnp.bfloat16)
        key_own = matmul(own_normed, w_key).astype(jnp.bfloat16)
        logits = matmul(own_normed, w_router).reshape(seg_len, 2 * H, E)
        gate_sig = jax.nn.sigmoid(logits)
        gate_vals = gate_sig * onehot
        projected = matmul(own_normed, w_value).reshape(seg_len, H, E, DH)
        value_own = (
            jnp.sum(gate_vals[:, :H, :, None] * projected, axis=2)
            .reshape(seg_len, H * DH)
            .astype(jnp.bfloat16)
        )
        return (queries, key_own, gate_sig, gate_vals, projected, value_own)

    queries, key_own, gate_sig, gate_vals, projected, value_own = projections()
    key_mem, value_mem = passed_along((key_own, value_own), "tm", 1)
    key_rows = jnp.concatenate([key_mem, key_own], axis=0)
    value_rows = jnp.concatenate([value_mem, value_own], axis=0)
    head_outs = []
    log_norms = []
    for head_idx in range(H):
        columns = slice(head_idx * DH, (head_idx + 1) * DH)
        scores = (
            jnp.einsum(
                "qd,kd->qk",
                queries[:, columns],
                key_rows[:, columns],
                preferred_element_type=jnp.float32,
            )
            * scale_factor
        )
        scores = jnp.where(allowed, scores, -1e30)
        peak = jnp.max(scores, axis=-1, keepdims=True)
        exp_scores = jnp.exp(scores - peak)
        total = jnp.sum(exp_scores, axis=-1, keepdims=True)
        weights = (exp_scores / total).astype(jnp.bfloat16)
        head_outs.append(matmul(weights, value_rows[:, columns]))
        log_norms.append(peak + jnp.log(total))
    attended = jnp.concatenate(head_outs, axis=1).astype(jnp.bfloat16)
    out_gates = gate_vals[:, H:]
    attended_f = attended.astype(jnp.float32).reshape(seg_len, H, 1, DH)
    mixed_in = (attended_f * out_gates[..., None]).reshape(seg_len, H * E * DH).astype(jnp.bfloat16)
    middle = own_rows + matmul(mixed_in, w_output)
    hidden_normed = normalize(middle, second_gain).astype(jnp.bfloat16)
    pre_act = matmul(hidden_normed, w_up)
    activated = exact_gelu(pre_act).astype(jnp.bfloat16)
    layer_out = middle + matmul(activated, w_down)
    output_block = layer_out.astype(jnp.bfloat16)[None]
    down_cot = output_cot[0]
    out_cot = down_cot.astype(jnp.float32)
    grad_down = tr_times(activated, down_cot)
    grad_act = times_tr(down_cot, w_down)
    unused_gelu, gelu_pull = jax.vjp(exact_gelu, pre_act)
    up_cot = gelu_pull(grad_act)[0].astype(jnp.bfloat16)
    grad_up = tr_times(hidden_normed, up_cot)
    normed_second_cot = times_tr(up_cot, w_up)
    unused_norm, second_pull = jax.vjp(normalize, middle, second_gain)
    middle_part, grad_second = second_pull(normed_second_cot)
    middle_cot = out_cot + middle_part
    branch_cot = middle_cot.astype(jnp.bfloat16)
    grad_output = tr_times(mixed_in, branch_cot)
    mixed_cot = times_tr(branch_cot, w_output).reshape(seg_len, H, E, DH)
    out_gate_cot = jnp.sum(mixed_cot * attended_f, axis=-1)
    attended_cot = (
        jnp.sum(mixed_cot * out_gates[..., None], axis=2)
        .reshape(seg_len, H * DH)
        .astype(jnp.bfloat16)
    )
    queries, key_own, gate_sig, gate_vals, projected, value_own = projections()
    key_back, value_back = passed_along((key_own, value_own), "tm", 1)
    key_rows = jnp.concatenate([key_back, key_own], axis=0)
    value_rows = jnp.concatenate([value_back, value_own], axis=0)
    query_grads = []
    key_grads = []
    value_grads = []
    for head_idx in range(H):
        columns = slice(head_idx * DH, (head_idx + 1) * DH)
        scores = (
            jnp.einsum(
                "qd,kd->qk",
                queries[:, columns],
                key_rows[:, columns],
                preferred_element_type=jnp.float32,
            )
            * scale_factor
        )
        scores = jnp.where(allowed, scores, -1e30)
        probs = jnp.exp(scores - log_norms[head_idx])
        weights = probs.astype(jnp.bfloat16)
        cot_head = attended_cot[:, columns]
        value_grads.append(tr_times(weights, cot_head))
        prob_cot = times_tr(cot_head, value_rows[:, columns])
        score_cot = (probs * (prob_cot - jnp.sum(probs * prob_cot, axis=-1, keepdims=True))).astype(
            jnp.bfloat16
        )
        query_grads.append(matmul(score_cot, key_rows[:, columns]) * scale_factor)
        key_grads.append(tr_times(score_cot, queries[:, columns]) * scale_factor)
    query_cot = jnp.concatenate(query_grads, axis=1).astype(jnp.bfloat16)
    key_cot_all = jnp.concatenate(key_grads, axis=1)
    value_cot_all = jnp.concatenate(value_grads, axis=1)
    key_mem_cot = key_cot_all[:seg_len].astype(jnp.bfloat16)
    key_own_cot = key_cot_all[seg_len:].astype(jnp.bfloat16)
    value_mem_cot = value_cot_all[:seg_len].astype(jnp.bfloat16)
    value_own_cot = value_cot_all[seg_len:].astype(jnp.bfloat16)
    key_next, value_next = passed_along((key_mem_cot, value_mem_cot), "tm", -1)
    own_vcot = value_own_cot.astype(jnp.float32).reshape(seg_len, H, 1, DH)
    next_vcot = value_next.astype(jnp.float32).reshape(seg_len, H, 1, DH)
    val_gates = gate_vals[:, :H, :, None]
    proj_own_cot = (val_gates * own_vcot).reshape(seg_len, H * E * DH).astype(jnp.bfloat16)
    proj_next_cot = (val_gates * next_vcot).reshape(seg_len, H * E * DH).astype(jnp.bfloat16)
    gate_own_cot = jnp.concatenate([jnp.sum(own_vcot * projected, axis=-1), out_gate_cot], axis=1)
    gate_next_cot = jnp.concatenate(
        [jnp.sum(next_vcot * projected, axis=-1), jnp.zeros_like(out_gate_cot)], axis=1
    )
    slope = gate_sig * (1.0 - gate_sig) * onehot
    logit_own_cot = (gate_own_cot * slope).reshape(seg_len, 2 * H * E).astype(jnp.bfloat16)
    logit_next_cot = (gate_next_cot * slope).reshape(seg_len, 2 * H * E).astype(jnp.bfloat16)
    twice_normed = jnp.concatenate([own_normed, own_normed], axis=0)
    key_both = jnp.concatenate([key_own_cot, key_next], axis=0)
    proj_both = jnp.concatenate([proj_own_cot, proj_next_cot], axis=0)
    logit_both = jnp.concatenate([logit_own_cot, logit_next_cot], axis=0)
    grad_query = tr_times(own_normed, query_cot)
    grad_key = tr_times(twice_normed, key_both)
    grad_value = tr_times(twice_normed, proj_both)
    grad_router = tr_times(twice_normed, logit_both)
    normed_both = (
        times_tr(key_both, w_key) + times_tr(proj_both, w_value) + times_tr(logit_both, w_router)
    )
    own_normed_cot = normed_both[:seg_len] + times_tr(query_cot, w_query)
    next_normed_cot = normed_both[seg_len:]
    grad_first = jnp.sum((own_normed_cot + next_normed_cot) * unit_normed, axis=0)
    unused_first, first_pull = jax.vjp(normalize, own_rows, first_gain)
    input_part = first_pull(own_normed_cot)[0]
    input_cot = middle_cot + input_part
    grad_gains = jnp.stack([grad_first, grad_second], axis=0)
    row_query, row_key, row_value, row_router, row_up = (
        lax.psum_scatter(grad_query, ("seq", "tm"), scatter_dimension=0, tiled=True),
        lax.psum_scatter(grad_key, ("seq", "tm"), scatter_dimension=0, tiled=True),
        lax.psum_scatter(grad_value, ("seq", "tm"), scatter_dimension=0, tiled=True),
        lax.psum_scatter(grad_router, ("seq", "tm"), scatter_dimension=0, tiled=True),
        lax.psum_scatter(grad_up, ("seq", "tm"), scatter_dimension=0, tiled=True),
    )
    col_gains, col_output, col_down = (
        lax.psum_scatter(grad_gains, ("seq", "tm"), scatter_dimension=1, tiled=True),
        lax.psum_scatter(grad_output, ("seq", "tm"), scatter_dimension=1, tiled=True),
        lax.psum_scatter(grad_down, ("seq", "tm"), scatter_dimension=1, tiled=True),
    )
    return (
        output_block,
        input_cot[None],
        col_gains,
        row_query,
        row_key,
        row_value,
        row_router,
        col_output,
        row_up,
        col_down,
    )


def solution(mesh):
    placed = (
        P("seq", "tm", None),
        P("seq", "tm", None, None),
        P("seq", "tm"),
        P(),
        P(),
        P(),
        P(),
        P(),
        P(),
        P(),
        P(),
        P("seq", "tm", None),
    )
    return jax.shard_map(
        per_device,
        mesh=mesh,
        in_specs=placed,
        out_specs=(
            P("seq", "tm", None),
            P("seq", "tm", None),
            P(None, ("seq", "tm")),
            P(("seq", "tm"), None),
            P(("seq", "tm"), None),
            P(("seq", "tm"), None),
            P(("seq", "tm"), None),
            P(None, ("seq", "tm")),
            P(("seq", "tm"), None),
            P(None, ("seq", "tm")),
        ),
        check_vma=False,
    )
```

profile of v0, /device:TPU:0, one launch (start us, length us, event | category | flops | bytes accessed | tf_op | source)
XLA Modules:
  0.0 1311.0 jit_solution(4716161394532378303)
XLA Ops:
  7.2 1.3 convert_reduce_fusion
  8.5 1.3 fusion.35
  9.9 0.8 fusion.135
  10.7 1.3 fusion.33
  12.5 2.4 collective-permute-start
  15.6 0.9 dot_general.155
  16.6 1.4 fusion.136
  18.1 3.9 multiply_reduce_fusion.4
  22.0 4.5 collective-permute-start.1
  31.9 1.5 fusion.141
  33.7 1.1 slice-done.1
  34.8 16.3 %multiply_convert_fusion = (bf16[256,4096]{1,0:T(8,128)(2,1)}, f32[256,4096]{1,0:T(8,128)}, f32[256,4096]{1,0:T(8,128)}) fusion(bf16[1024,4096]{1,0:T(8,128)(2,1)S(1)} %bitcast.173, f32[256,1024]{1,0:T(8,128)S(1)} %get-tuple-element.47, f32[1024]{0:T(1024)S(1)} %bitcast.157, f32[256]{0:T(256)S(1)} %fusion.105, f32[256]{0:T(256)S(1)} %broadcast_multiply_fusion), kind=kOutput, calls=%fused_computation.3 | convolution fusion | flops 2216689664 | bytes 19929088 | tf_op jit(solution)/shard_map/dot_general | solution.py:31
  51.1 11.3 add_convert_fusion
  62.4 7.3 multiply_reduce_fusion.5
  70.4 4.0 fusion.142
  75.6 0.8 fusion.25
  77.7 1.5 collective-permute-start.3
  81.4 0.8 fusion.132
  82.2 1.4 collective-permute-start.2
  83.6 0.8 fusion.24
  84.5 0.8 fusion.23
  85.3 0.8 fusion.22
  86.2 2.3 multiply_reduce_fusion
  89.8 1.4 convert_element_type.188
  91.1 1.3 copy.47
  92.5 1.4 convert_element_type.186
  95.3 5.2 fusion.7
  101.1 1.8 add_add_fusion
  103.7 1.2 fusion.34
  105.5 1.7 copy.51
  107.3 2.5 fusion.40
  109.8 2.8 fusion.102
  112.8 3.4 fusion.41
  116.2 6.4 fusion.144
  122.7 8.2 fusion.6
  131.3 9.8 fusion.128
  141.2 9.8 fusion.45
  151.0 7.2 fusion.19
  158.3 1.5 add_bitcast_fusion
  159.8 85.8 %reduce-scatter.25.cloned.1.call-done = f32[32,2]{1,0:T(8,128)} async-done(((f32[1024,2]{1,0:T(8,128)}), f32[32,2]{1,0:T(8,128)}) %reduce-scatter.25.cloned.1.call-update) | async-done | bytes 272
  245.6 1.4 copy.52
  247.0 131.5 %reduce-scatter.17.cloned.1.call-done = f32[32,40]{1,0:T(8,128)} async-done(((f32[1024,40]{1,0:T(8,128)}), f32[32,40]{1,0:T(8,128)}) %reduce-scatter.17.cloned.1.call-update) | async-done | bytes 5136 | tf_op jit(solution)/shard_map/reduce_scatter | solution.py:225
  378.5 136.0 %reduce-scatter.11.cloned.1.call-done = f32[32,448]{1,0:T(8,128)} async-done(((f32[1024,448]{1,0:T(8,128)}), f32[32,448]{1,0:T(8,128)}) %reduce-scatter.11.cloned.1.call-update) | async-done | bytes 57360 | tf_op jit(solution)/shard_map/reduce_scatter | solution.py:222
  514.5 135.9 %reduce-scatter.13.cloned.1.call-done = f32[32,448]{1,0:T(8,128)} async-done(((f32[1024,448]{1,0:T(8,128)}), f32[32,448]{1,0:T(8,128)}) %reduce-scatter.13.cloned.1.call-update) | async-done | bytes 57360 | tf_op jit(solution)/shard_map/reduce_scatter | solution.py:223
  650.4 138.1 %reduce-scatter.19.cloned.1.call-done = f32[2240,32]{0,1:T(8,128)} async-done(((f32[2240,1024]{0,1:T(8,128)}), f32[2240,32]{0,1:T(8,128)}) %reduce-scatter.19.cloned.1.call-update) | async-done | bytes 286736 | tf_op jit(solution)/shard_map/reduce_scatter | solution.py:230
  788.5 142.1 %reduce-scatter.15.cloned.1.call-done = f32[32,2240]{1,0:T(8,128)} async-done(((f32[1024,2240]{1,0:T(8,128)}), f32[32,2240]{1,0:T(8,128)}) %reduce-scatter.15.cloned.1.call-update) | async-done | bytes 286736 | tf_op jit(solution)/shard_map/reduce_scatter | solution.py:224
  930.6 185.6 %reduce-scatter.21.cloned.1.call-done = f32[32,4096]{1,0:T(8,128)} async-done(((f32[1024,4096]{1,0:T(8,128)}), f32[32,4096]{1,0:T(8,128)}) %reduce-scatter.21.cloned.1.call-update) | async-done | bytes 524304 | tf_op jit(solution)/shard_map/reduce_scatter | solution.py:226
  1116.2 187.6 %reduce-scatter.23.cloned.1.call-done = f32[4096,32]{0,1:T(8,128)} async-done(((f32[4096,1024]{0,1:T(8,128)}), f32[4096,32]{0,1:T(8,128)}) %reduce-scatter.23.cloned.1.call-update) | async-done | bytes 524304 | tf_op jit(solution)/shard_map/reduce_scatter | solution.py:231
  (175 shorter events, 16.3 us)
Async XLA Ops:
  7.2 4.8 copy-start
  7.2 10.9 copy-start.1
  7.2 238.4 %reduce-scatter.25.cloned.1.call-start = ((), (), s32[]{:S(2)}) async-start(), calls=%async_computation.15 | async-start | bytes 540672
  9.9 2.1 copy-start.33
  9.9 12.1 copy-start.26
  12.0 15.2 %copy-start.2 = (bf16[256,1024]{1,0:T(8,128)(2,1)}, bf16[256,1024]{1,0:T(8,128)(2,1)S(1)}, u32[]{:S(2)}) copy-start(bf16[256,1024]{1,0:T(8,128)(2,1)S(1)} %fusion.33) | copy-start | bytes 1572868
  12.5 17.1 %copy-start.4 = (bf16[256,448]{0,1:T(8,128)(2,1)}, bf16[256,448]{0,1:T(8,128)(2,1)S(1)}, u32[]{:S(2)}) copy-start(bf16[256,448]{0,1:T(8,128)(2,1)S(1)} %convolution_convert_fusion) | copy-start | bytes 688132
  12.5 15.2 %collective-permute-start = (bf16[256,448]{0,1:T(8,128)(2,1)S(1)}, bf16[256,448]{0,1:T(8,128)(2,1)S(1)}, u32[]{:S(2)}, u32[]{:S(2)}) collective-permute-start(bf16[256,448]{0,1:T(8,128)(2,1)S(1)} %convolution_convert_fusion), channel_id=1, source_target_pairs={{0,1},{1,2},{2,3},{3,4},{4,5},{5,6},{6,7},{7,8},{8,9},{9,10},{10,1... | collective-permute-start | bytes 688136 | tf_op jit(solution)/shard_map/ppermute | solution.py:17
  15.6 2.4 copy-start.22
  18.1 9.2 copy-start.14
  22.0 8.2 collective-permute-start.1
  27.8 2.8 copy-start.10
  29.3 2.5 slice-start.2
  30.9 2.8 slice-start
  31.9 2.9 slice-start.1
  33.6 36.1 %copy-start.25 = (f32[256]{0:T(256)}, f32[256]{0:T(256)S(1)}, u32[]{:S(2)}) copy-start(f32[256]{0:T(256)S(1)} %fusion.105) | copy-start | bytes 3076
  34.8 16.3 %copy-start.6 = (bf16[1,256,1024]{2,1,0:T(8,128)(2,1)S(1)}, bf16[1,256,1024]{2,1,0:T(8,128)(2,1)}, u32[]{:S(2)}) copy-start(bf16[1,256,1024]{2,1,0:T(8,128)(2,1)} %param.23) | copy-start | bytes 1572868
  62.4 7.3 copy-start.12
  70.2 4.2 copy-start.31
  70.4 4.0 copy-start.13
  77.7 8.5 collective-permute-start.3
  79.9 3.7 copy-start.5
  79.9 3.7 copy-start.11
  82.2 6.3 copy-start.23
  82.2 18.9 %collective-permute-start.2 = (bf16[256,448]{0,1:T(8,128)(2,1)}, bf16[256,448]{0,1:T(8,128)(2,1)}, u32[]{:S(2)}, u32[]{:S(2)}) collective-permute-start(bf16[256,448]{0,1:T(8,128)(2,1)} %get-tuple-element.23), channel_id=1, source_target_pairs={{1,0},{2,1},{3,2},{4,3},{5,4},{6,5},{7,6},{8,7},{9,8},{10,9},{11,1... | collective-permute-start | bytes 688136 | tf_op jit(solution)/shard_map/ppermute | solution.py:17
  95.3 5.2 copy-start.24
  95.3 5.2 copy-start.17
  95.3 5.8 copy-start.16
  101.0 1.9 copy-start.15
  101.0 1.9 copy-start.18
  101.0 1.9 copy-start.19
  101.0 1.9 copy-start.20
  101.1 1.9 copy-start.21
  101.1 2.5 copy-start.34
  101.1 2.6 copy-start.27
  107.2 271.3 %reduce-scatter.17.cloned.1.call-start = ((), (), s32[]{:S(2)}) async-start(), calls=%async_computation.11 | async-start | bytes 540672 | tf_op jit(solution)/shard_map/reduce_scatter | solution.py:225
  109.8 404.7 %reduce-scatter.11.cloned.1.call-start = ((), (), s32[]{:S(2)}) async-start(), calls=%async_computation.8 | async-start | bytes 2162688 | tf_op jit(solution)/shard_map/reduce_scatter | solution.py:222
  112.7 537.7 %reduce-scatter.13.cloned.1.call-start = ((), (), s32[]{:S(2)}) async-start(), calls=%async_computation.9 | async-start | bytes 2162688 | tf_op jit(solution)/shard_map/reduce_scatter | solution.py:223
  116.2 672.3 %reduce-scatter.19.cloned.1.call-start = ((), (), s32[]{:S(2)}) async-start(), calls=%async_computation.12 | async-start | bytes 9732096 | tf_op jit(solution)/shard_map/reduce_scatter | solution.py:230
  122.7 807.9 %reduce-scatter.15.cloned.1.call-start = ((), (), s32[]{:S(2)}) async-start(), calls=%async_computation.10 | async-start | bytes 9732096 | tf_op jit(solution)/shard_map/reduce_scatter | solution.py:224
  131.0 985.2 %reduce-scatter.21.cloned.1.call-start = ((), (), s32[]{:S(2)}) async-start(), calls=%async_computation.13 | async-start | bytes 17301504 | tf_op jit(solution)/shard_map/reduce_scatter | solution.py:226
  141.1 1162.6 %reduce-scatter.23.cloned.1.call-start = ((), (), s32[]{:S(2)}) async-start(), calls=%async_computation.14 | async-start | bytes 17301504 | tf_op jit(solution)/shard_map/reduce_scatter | solution.py:231
  151.0 7.3 copy-start.35
  151.0 7.3 copy-start.7
  151.0 7.3 copy-start.9
  151.0 7.3 copy-start.28
  151.0 7.3 copy-start.30
  151.0 7.3 copy-start.32
  (5 other events, 7.1 us)
Sparse Core Ops, SparseCore 0:
  107.3 138.2 reduce-scatter.24
  248.5 129.9 reduce-scatter.16
  381.3 133.1 reduce-scatter.10
  517.3 133.0 reduce-scatter.12
  656.8 131.7 reduce-scatter.18
  795.8 134.6 reduce-scatter.14
  933.4 182.6 reduce-scatter.20
  1119.0 184.6 reduce-scatter.22
where the time goes:
time: 1320 us; the launch traced here: 1310 us
  waiting for transfers between devices  1140 us (86%)
  matrix products  114 us (9%)
  between operations  16.2 us (1%)
  local copies, waits for them, and re-layouts  13.9 us (1%)
  other arithmetic  13.4 us (1%)
    reduce_scatter x1, waiting for transfers between devices, per_device(): lax.psum_scatter(grad_down, ('seq', 'tm'), scatter_dimension=1, tiled=True)  188 us
    reduce_scatter x1, waiting for transfers between devices, per_device(): lax.psum_scatter(grad_up, ('seq', 'tm'), scatter_dimension=0, tiled=True)  186 us
    reduce_scatter x1, waiting for transfers between devices, per_device(): lax.psum_scatter(grad_value, ('seq', 'tm'), scatter_dimension=0, tiled=True)  142 us
    reduce_scatter x1, waiting for transfers between devices, per_device(): lax.psum_scatter(grad_output, ('seq', 'tm'), scatter_dimension=1, tiled=T...  138 us
    reduce_scatter x1, waiting for transfers between devices, per_device(): lax.psum_scatter(grad_query, ('seq', 'tm'), scatter_dimension=0, tiled=True)  136 us
    reduce_scatter x1, waiting for transfers between devices, per_device(): lax.psum_scatter(grad_key, ('seq', 'tm'), scatter_dimension=0, tiled=True)  136 us
    reduce_scatter x1, waiting for transfers between devices, per_device(): lax.psum_scatter(grad_router, ('seq', 'tm'), scatter_dimension=0, tiled=T...  131 us
    unnamed x9, waiting for transfers between devices  85.9 us
  transfers between devices with their start and end apart: 12, of which 8 were waited for; matrix products, arithmetic and copies ran while one was open for 6% of the time, Pallas kernels for 0%

commit v1 on v0

--- a/solution.py
+++ b/solution.py
@@ -1,6 +1,12 @@
+import types
+
 import jax
 import jax.numpy as jnp
+import ml_dtypes
+import numpy as np
 from jax import lax
+from jax.experimental import pallas as pl
+from jax.experimental.pallas import tpu as pltpu
 from jax.sharding import PartitionSpec as P
 
 H = 4
@@ -244,6 +250,897 @@
     )
 
 
+VMEM_LIMIT = 64 << 20
+
+MESH_ID = pl.DeviceIdType.MESH
+NS = 12
+TILE = 128
+AB_T = 7
+C_T = 2
+PER = AB_T + C_T
+AB_W = AB_T * TILE
+C_W = C_T * TILE
+FLAT = NS * PER * TILE
+NR = 4
+NZ = 6
+FIRST = slice(0, AB_W)
+LAST = slice(AB_W, AB_W + C_W)
+HALF = (slice(0, 16), slice(16, 32))
+
+
+def rem(a, n):
+    return a % n if isinstance(a, int) else lax.rem(a, n)
+
+
+def place():
+    s = lax.axis_index("seq")
+    t = lax.axis_index("tm")
+    return s, t, t // 4, (t // 2) % 2, t % 2
+
+
+def store_tile(parts, tile, value):
+    piece = tile // PER
+    slot = tile - piece * PER
+    at = slot * TILE
+    cols = slice(at, at + TILE) if isinstance(at, int) else pl.ds(pl.multiple_of(at, TILE), TILE)
+    parts[piece, :, :, :, :, cols] = value.reshape(2, 4, 2, 32, TILE).astype(jnp.bfloat16)
+
+
+class Exchange:
+    def __init__(self, parts, bufs, sems, stage, out_sem, out):
+        self.parts, self.out = parts, out
+        self.stage, self.out_sem = stage, out_sem
+        (self.xa, self.yb, self.ya, self.xb, self.zu, self.zd, self.zuc, self.zdc, self.xc, self.yc) = bufs
+        self.ssem, self.rsem = sems
+        self.s, self.t, self.z, self.y, self.c = place()
+        s, t = self.s, self.t
+        self.to_x = {"seq": 1 - s, "tm": t}
+        self.to_y = {"seq": s, "tm": t + 2 - 4 * self.y}
+        self.to_up = {"seq": s, "tm": t + 4}
+        self.to_down = {"seq": s, "tm": t - 4}
+
+    def copy(self, kind, piece, src, dst, dev):
+        return pltpu.make_async_remote_copy(
+            src_ref=src, dst_ref=dst, send_sem=self.ssem.at[kind, piece],
+            recv_sem=self.rsem.at[kind, piece], device_id=dev, device_id_type=MESH_ID)
+
+    def c_xa(self, p):
+        return self.copy(0, p, self.parts.at[p, 1 - self.s, :, :, HALF[0], FIRST], self.xa.at[rem(p, NR)], self.to_x)
+
+    def c_yb(self, p):
+        return self.copy(1, p, self.parts.at[p, :, :, 1 - self.y, HALF[1], FIRST], self.yb.at[rem(p, NR)], self.to_y)
+
+    def c_ya(self, p):
+        return self.copy(2, p, self.parts.at[p, self.s, :, 1 - self.y, HALF[0], FIRST], self.ya.at[rem(p, NR)], self.to_y)
+
+    def c_xb(self, p):
+        return self.copy(3, p, self.parts.at[p, 1 - self.s, :, self.y, HALF[1], FIRST], self.xb.at[rem(p, NR)], self.to_x)
+
+    def c_xc(self, p):
+        return self.copy(4, p, self.parts.at[p, 1 - self.s, self.z, :, :, LAST], self.xc.at[rem(p, NR)], self.to_x)
+
+    def c_yc(self, p):
+        return self.copy(5, p, self.parts.at[p, self.s, self.z, 1 - self.y, :, LAST], self.yc.at[rem(p, NR)], self.to_y)
+
+    def c_up(self, p, z):
+        return self.copy(6, p, self.parts.at[p, self.s, z + 1:4, self.y, :, FIRST], self.zu.at[rem(p, NZ), z:3], self.to_up)
+
+    def c_down(self, p, z):
+        return self.copy(7, p, self.parts.at[p, self.s, 0:z, self.y, :, FIRST], self.zd.at[rem(p, NZ), 0:z], self.to_down)
+
+    def c_upc(self, p, z):
+        return self.copy(8, p, self.parts.at[p, :, z + 1:4, :, :, LAST], self.zuc.at[rem(p, NZ), :, z:3], self.to_up)
+
+    def c_downc(self, p, z):
+        return self.copy(9, p, self.parts.at[p, :, 0:z, :, :, LAST], self.zdc.at[rem(p, NZ), :, 0:z], self.to_down)
+
+    def z_step(self, p, k, is_c):
+        up, down = (self.c_upc, self.c_downc) if is_c else (self.c_up, self.c_down)
+
+        def add(u, src, at):
+            if is_c:
+                def body(i, _):
+                    a, b = i // 2, i % 2
+                    self.parts[p, a, u, b, :, LAST] = self.parts[p, a, u, b, :, LAST] + src[rem(p, NZ), a, at, b]
+                    return 0
+                lax.fori_loop(0, 4, body, 0)
+            else:
+                self.parts[p, self.s, u, self.y, :, FIRST] = self.parts[p, self.s, u, self.y, :, FIRST] + src[rem(p, NZ), at]
+
+        @pl.when(self.z == k - 1)
+        def _():
+            z = k - 1
+            if z > 0:
+                up(p, z - 1).wait_recv()
+                for u in range(z + 1, 4):
+                    add(u, self.zuc if is_c else self.zu, u - 1)
+            if z < 3:
+                up(p, z).start()
+
+        @pl.when(self.z == 4 - k)
+        def _():
+            z = 4 - k
+            if z < 3:
+                down(p, z + 1).wait_recv()
+                for u in range(0, z):
+                    add(u, self.zdc if is_c else self.zd, u)
+            if z > 0:
+                down(p, z).start()
+
+    def step1_ab(self, p):
+        self.c_xa(p).start()
+        self.c_yb(p).start()
+
+    def step1(self, p):
+        if isinstance(p, int):
+            if p > 0:
+                self.step1_ab(p)
+        else:
+            pl.when(p > 0)(lambda: self.step1_ab(p))
+        self.z_step(p, 1, True)
+
+    def step2(self, p):
+        self.c_xa(p).wait_recv()
+
+        def body(i, _):
+            a, b = i // 2, i % 2
+            self.parts[p, self.s, a, b, HALF[0], FIRST] = self.parts[p, self.s, a, b, HALF[0], FIRST] + self.xa[rem(p, NR), a, b]
+            return 0
+        lax.fori_loop(0, 8, body, 0)
+        self.c_ya(p).start()
+        self.c_yb(p).wait_recv()
+
+        def body(i, _):
+            a, b = i // 4, i % 4
+            self.parts[p, a, b, self.y, HALF[1], FIRST] = self.parts[p, a, b, self.y, HALF[1], FIRST] + self.yb[rem(p, NR), a, b]
+            return 0
+        lax.fori_loop(0, 8, body, 0)
+        self.c_xb(p).start()
+        self.z_step(p, 2, True)
+
+    def step3(self, p):
+        self.c_ya(p).wait_recv()
+        self.c_xb(p).wait_recv()
+
+        def body(b, _):
+            self.parts[p, self.s, b, self.y, HALF[0], FIRST] = self.parts[p, self.s, b, self.y, HALF[0], FIRST] + self.ya[rem(p, NR), b]
+            self.parts[p, self.s, b, self.y, HALF[1], FIRST] = self.parts[p, self.s, b, self.y, HALF[1], FIRST] + self.xb[rem(p, NR), b]
+            return 0
+        lax.fori_loop(0, 4, body, 0)
+        self.z_step(p, 1, False)
+        self.z_step(p, 3, True)
+
+    def step4(self, p):
+        self.z_step(p, 2, False)
+        self.z_step(p, 4, True)
+        z = self.z
+
+        @pl.when(z > 0)
+        def _():
+            def body(i, _):
+                a, b = i // 2, i % 2
+                self.parts[p, a, z, b, :, LAST] = self.parts[p, a, z, b, :, LAST] + self.zuc[rem(p, NZ), a, z - 1, b]
+                return 0
+            lax.fori_loop(0, 4, body, 0)
+
+        @pl.when(z < 3)
+        def _():
+            def body(i, _):
+                a, b = i // 2, i % 2
+                self.parts[p, a, z, b, :, LAST] = self.parts[p, a, z, b, :, LAST] + self.zdc[rem(p, NZ), a, z, b]
+                return 0
+            lax.fori_loop(0, 4, body, 0)
+        self.c_xc(p).start()
+
+    def step5(self, p):
+        self.z_step(p, 3, False)
+        self.c_xc(p).wait_recv()
+        for b in range(2):
+            self.parts[p, self.s, self.z, b, :, LAST] = self.parts[p, self.s, self.z, b, :, LAST] + self.xc[rem(p, NR), b]
+        self.c_yc(p).start()
+
+    def step6(self, p):
+        self.z_step(p, 4, False)
+        z = self.z
+        k = p % 2
+
+        @pl.when(p >= 2)
+        def _():
+            self.c_out(p - 2).wait()
+        cols, colc = slice(0, AB_W), slice(AB_W, AB_W + C_W)
+        mine = self.parts[p, self.s, z, self.y, :, FIRST].astype(jnp.float32)
+
+        @pl.when(z == 0)
+        def _():
+            self.stage[k, :, cols] = mine + self.zd[rem(p, NZ), 0].astype(jnp.float32)
+
+        @pl.when(z == 3)
+        def _():
+            self.stage[k, :, cols] = mine + self.zu[rem(p, NZ), 2].astype(jnp.float32)
+
+        @pl.when((z > 0) & (z < 3))
+        def _():
+            self.stage[k, :, cols] = (mine + self.zu[rem(p, NZ), z - 1].astype(jnp.float32)) + self.zd[rem(p, NZ), z].astype(jnp.float32)
+        self.c_yc(p).wait_recv()
+        self.stage[k, :, colc] = self.parts[p, self.s, z, self.y, :, LAST].astype(jnp.float32) + self.yc[rem(p, NR)].astype(jnp.float32)
+        self.c_out(p).start()
+
+    def c_out(self, p):
+        cols = pl.ds(pl.multiple_of(p * (PER * TILE), TILE), PER * TILE)
+        return pltpu.make_async_copy(self.stage.at[p % 2], self.out.at[:, cols], self.out_sem.at[p % 2])
+
+    def tick(self, t):
+        steps = (self.step1, self.step2, self.step3, self.step4, self.step5, self.step6)
+        for k, step in enumerate(steps):
+            p = t - k
+            if isinstance(t, int):
+                if 0 <= p < NS:
+                    step(p)
+            else:
+                @pl.when((p >= 0) & (p < NS))
+                def _(step=step, p=p):
+                    step(p)
+
+    def finish(self):
+        self.c_out(NS - 2).wait()
+        self.c_out(NS - 1).wait()
+
+        def body(p, _):
+            self.c_xa(p).wait_send()
+            self.c_yb(p).wait_send()
+            self.c_ya(p).wait_send()
+            self.c_xb(p).wait_send()
+            self.c_xc(p).wait_send()
+            self.c_yc(p).wait_send()
+            for z in range(4):
+                @pl.when(self.z == z)
+                def _(z=z):
+                    if z < 3:
+                        self.c_up(p, z).wait_send()
+                        self.c_upc(p, z).wait_send()
+                    if z > 0:
+                        self.c_down(p, z).wait_send()
+                        self.c_downc(p, z).wait_send()
+            return 0
+        lax.fori_loop(0, NS, body, 0)
+
+
+P_SCRATCH = [pltpu.VMEM((NS, 2, 4, 2, 32, PER * TILE), jnp.bfloat16)]
+RECV_SCRATCH = [
+    pltpu.VMEM((NR, 4, 2, 16, AB_W), jnp.bfloat16),
+    pltpu.VMEM((NR, 2, 4, 16, AB_W), jnp.bfloat16),
+    pltpu.VMEM((NR, 4, 16, AB_W), jnp.bfloat16),
+    pltpu.VMEM((NR, 4, 16, AB_W), jnp.bfloat16),
+    pltpu.VMEM((NZ, 3, 32, AB_W), jnp.bfloat16),
+    pltpu.VMEM((NZ, 3, 32, AB_W), jnp.bfloat16),
+    pltpu.VMEM((NZ, 2, 3, 2, 32, C_W), jnp.bfloat16),
+    pltpu.VMEM((NZ, 2, 3, 2, 32, C_W), jnp.bfloat16),
+    pltpu.VMEM((NR, 2, 32, C_W), jnp.bfloat16),
+    pltpu.VMEM((NR, 32, C_W), jnp.bfloat16),
+]
+
+
+def greet():
+    s, t, z, y, c = place()
+    bar = pltpu.get_barrier_semaphore()
+
+    def tell(dev):
+        pl.semaphore_signal(bar, inc=1, device_id=dev, device_id_type=MESH_ID)
+    tell({"seq": 1 - s, "tm": t})
+    tell({"seq": s, "tm": t + 2 - 4 * y})
+    tell({"seq": s, "tm": t + 1 - 2 * c})
+
+    @pl.when(z < 3)
+    def _():
+        tell({"seq": s, "tm": t + 4})
+
+    @pl.when(z > 0)
+    def _():
+        tell({"seq": s, "tm": t - 4})
+    far = jnp.where(c == 1, t + 1, t - 1)
+    has_far = (far >= 0) & (far < 16)
+
+    @pl.when(has_far)
+    def _():
+        tell({"seq": s, "tm": far})
+    return bar, 3 + jnp.where(has_far, 1, 0) + jnp.where(z < 3, 1, 0) + jnp.where(z > 0, 1, 0)
+
+
+D = 1024
+FF = 4096
+SEG = 256
+HD = H * DH
+WIDE = H * E * DH
+FFB = 512
+NFF = FF // FFB
+NG = 4
+WB = 512
+LOGIT = 64
+OWN_SIB = 24
+F32 = jnp.float32
+BF = jnp.bfloat16
+
+
+def dot(a, b):
+    return jnp.dot(a, b, preferred_element_type=F32)
+
+
+def dot_nt(a, b):
+    return lax.dot_general(a, b, (((1,), (1,)), ((), ())), preferred_element_type=F32)
+
+
+def dot_tn(a, b):
+    return lax.dot_general(a, b, (((0,), (0,)), ((), ())), preferred_element_type=F32)
+
+
+def halves(v):
+    top = v.astype(BF)
+    return top, (v - top.astype(F32)).astype(BF)
+
+
+def unit_rows(v):
+    centre = v - jnp.mean(v, axis=-1, keepdims=True)
+    spread = jnp.mean(centre * centre, axis=-1, keepdims=True)
+    inv = lax.rsqrt(spread + epsilon)
+    return centre * inv, inv
+
+
+def norm_back(unit, inv, cot):
+    return inv * (cot - jnp.mean(cot, axis=-1, keepdims=True)
+                  - unit * jnp.mean(cot * unit, axis=-1, keepdims=True))
+
+
+def for_rows(step, body):
+    def inner(i, _):
+        body(pl.ds(pl.multiple_of(i * step, step), step))
+        return 0
+    lax.fori_loop(0, SEG // step, inner, 0)
+
+
+def for_wide(body):
+    whole = WIDE // WB
+
+    def inner(i, _):
+        body(pl.ds(pl.multiple_of(i * WB, WB), WB), i * WB)
+        return 0
+    lax.fori_loop(0, whole, inner, 0)
+    body(slice(whole * WB, WIDE), whole * WB)
+
+
+NAMES = (
+    "x", "oc", "gains", "rt", "rf", "spread", "hot", "wq", "wk", "wr", "wrp", "wu", "wd", "sel", "exv", "exo",
+    "xn", "hn", "mid", "lo", "nsc", "q", "k", "v", "sig", "att", "acc", "g_o", "g_p",
+    "act", "uc", "bc", "kc", "vc", "kn", "vn", "ob", "gg", "ogc", "qc",
+    "at", "full",
+    "ld", "ld2", "kv_s", "kv_r", "sib_s", "sib_r", "st", "stage", "out_sem", "ssem", "rsem",
+)
+
+
+def layer_scratch():
+    dma = pltpu.SemaphoreType.DMA
+    v = pltpu.VMEM
+    return [
+        v((SEG, D), BF), v((SEG, D), BF), v((2, D), BF), v((2 * H, 2, SEG), jnp.int32), v((128, SEG), BF),
+        v((128, 256), BF), v((SEG, 128), F32),
+        v((HD, D), BF), v((HD, D), BF), v((2 * H * E, D), BF), v((128, D), BF),
+        v((2, D, FFB), BF), v((2, FFB, D), BF), v((WIDE, 512), BF), v((256, 2304), BF), v((256, 2304), BF),
+        v((SEG, D), BF), v((SEG, D), BF), v((SEG, D), F32), v((SEG, D), F32), v((SEG, D), F32),
+        v((SEG, HD), BF), v((2 * SEG, HD), BF), v((2 * SEG, HD), BF), v((SEG, 128), F32),
+        v((SEG, HD), BF), v((2 * SEG, HD), F32), v((2 * SEG, 2304), BF), v((2 * SEG, 3328), BF),
+        v((NG, 2 * SEG, FFB), BF), v((NG, 2 * SEG, FFB), BF), v((SEG, D), BF),
+        v((2 * SEG, HD), BF), v((2 * SEG, HD), BF), v((SEG, HD), BF), v((SEG, HD), BF), v((SEG, D), BF), v((SEG, 256), BF), v((SEG, 128), F32), v((SEG, HD), F32),
+        v((6, 16, 32, 2 * SEG), BF), v((2, 16, 2, 32, SEG), BF),
+        dma((16,)), dma((4,)), dma((4,)), dma((4,)), dma((OWN_SIB,)), dma((OWN_SIB,)), dma((2,)),
+        v((2, 32, PER * TILE), F32), dma((2,)), dma((10, NS)), dma((10, NS)),
+    ]
+
+
+def layer_kernel(x_h, rt_h, len_s, gains_h, wq_h, wk_h, wv_h, wr_h, wo_h, wu_h, wd_h, oc_h,
+                 sel_h, exv_h, exo_h, spread_h, lo_h, ig_h, flat_h, *scratch):
+    m = types.SimpleNamespace(**dict(zip(NAMES, scratch[:len(NAMES)])))
+    recv = scratch[len(NAMES):]
+    s, t, z, y, c = place()
+    last_t = lax.axis_size("tm") - 1
+    sib = {"seq": s, "tm": t + 1 - 2 * c}
+    scale = DH ** -0.5
+    own = slice(SEG, 2 * SEG)
+    mem = slice(0, SEG)
+
+    bar, peers = greet()
+
+    def load(i, src, dst):
+        cp = pltpu.make_async_copy(src, dst, m.ld.at[i])
+        cp.start()
+        return cp
+
+    def sibling(i, src, dst):
+        return pltpu.make_async_remote_copy(
+            src_ref=src, dst_ref=dst, send_sem=m.sib_s.at[i], recv_sem=m.sib_r.at[i],
+            device_id=sib, device_id_type=MESH_ID)
+
+    def at_copy(i, slot):
+        return sibling(i, m.full.at[slot, :, 1 - c], m.at.at[i, :, :, SEG:])
+
+    def turn(i, slot, value):
+        m.full[slot] = jnp.transpose(value).reshape(16, 2, 32, SEG)
+        m.at[i, :, :, :SEG] = m.full[slot, :, c]
+        at_copy(i, slot).start()
+
+    def go_copy():
+        return sibling(6, m.g_o.at[mem], m.g_o.at[own])
+
+    def gp_copy():
+        return sibling(7, m.g_p.at[mem], m.g_p.at[own])
+
+    def ff_copies(j):
+        g = rem(j, NG)
+        return (sibling(8 + 2 * j, m.act.at[g, mem], m.act.at[g, own]),
+                sibling(9 + 2 * j, m.uc.at[g, mem], m.uc.at[g, own]))
+
+    def ff_loads(j):
+        cols = pl.ds(pl.multiple_of(j * FFB, FFB), FFB)
+        return (pltpu.make_async_copy(wu_h.at[:, cols], m.wu.at[j % 2], m.ld2.at[j % 2]),
+                pltpu.make_async_copy(wd_h.at[cols, :], m.wd.at[j % 2], m.ld2.at[2 + j % 2]))
+
+    def along(i, src, dst, by):
+        return pltpu.make_async_remote_copy(
+            src_ref=src, dst_ref=dst, send_sem=m.kv_s.at[i], recv_sem=m.kv_r.at[i],
+            device_id={"seq": s, "tm": t + by}, device_id_type=MESH_ID)
+
+    def k_copy():
+        return along(0, m.k.at[own], m.k.at[mem], 1)
+
+    def v_copy():
+        return along(1, m.v.at[own], m.v.at[mem], 1)
+
+    def kc_copy():
+        return along(2, m.kc.at[mem], m.kn, -1)
+
+    def vc_copy():
+        return along(3, m.vc.at[mem], m.vn, -1)
+
+    def head_lanes(rows, h):
+        lane = lax.broadcasted_iota(jnp.int32, (rows, HD), 1)
+        return (lane >= h * DH) & (lane < (h + 1) * DH)
+
+    def head_only(v, h):
+        return jnp.where(head_lanes(v.shape[0], h), v, jnp.zeros_like(v))
+
+    def gates_wide(table, cols):
+        return dot(m.gg[...], table[:, cols])
+
+    def weights_of(h):
+        scores = dot_nt(head_only(m.q[...], h), m.k[...]) * scale
+        length = len_s[0, 0]
+        row = lax.broadcasted_iota(jnp.int32, (SEG, 2 * SEG), 0)
+        col = lax.broadcasted_iota(jnp.int32, (SEG, 2 * SEG), 1)
+        allowed = ((col < SEG) & (col >= SEG - length)) | ((col >= SEG) & (col - SEG <= row))
+        scores = jnp.where(allowed, scores, -1e30)
+        e = jnp.exp(scores - jnp.max(scores, axis=-1, keepdims=True))
+        return e / jnp.sum(e, axis=-1, keepdims=True)
+
+    l_x = load(0, x_h, m.x)
+    l_g = load(1, gains_h, m.gains)
+    l_k = load(2, wk_h, m.wk)
+    l_r = load(3, wr_h, m.wr)
+    l_rt = load(4, rt_h, m.rt)
+    l_sp = load(12, spread_h, m.spread)
+
+    def forward(wv, wo):
+        l_v = load(5, wv_h, wv)
+        l_ev = load(6, exv_h, m.exv)
+        l_sel = load(7, sel_h, m.sel)
+        l_x.wait()
+        l_g.wait()
+
+        def norm1(rows):
+            unit, _ = unit_rows(m.x[rows, :].astype(F32))
+            m.xn[rows, :] = (unit * m.gains[0:1, :].astype(F32)).astype(BF)
+        for_rows(32, norm1)
+        l_k.wait()
+        m.k[own, :] = dot_nt(m.xn[...], m.wk[...]).astype(BF)
+        l_q = load(8, wq_h, m.wq)
+        l_oc = load(9, oc_h, m.oc)
+        l_eo = load(10, exo_h, m.exo)
+        l_wo = load(11, wo_h, wo)
+        for j in range(2):
+            for cp in ff_loads(j):
+                cp.start()
+        pl.semaphore_wait(bar, peers)
+
+        @pl.when(t < last_t)
+        def _():
+            k_copy().start()
+        l_r.wait()
+        m.wrp[...] = jnp.zeros((128, D), BF)
+        m.wrp[LOGIT:LOGIT + 2 * H * E, :] = m.wr[...]
+        sig = jax.nn.sigmoid(dot_nt(m.xn[...], m.wrp[...]))
+        l_rt.wait()
+        l_sp.wait()
+        m.rf[...] = jnp.zeros((128, SEG), BF)
+        for i in range(2):
+            m.rf[16 * i:16 * i + 2 * H, :] = m.rt[:, i, :].astype(F32).astype(BF)
+        named = dot_tn(m.rf[...], m.spread[...])
+        expert = m.spread[127:128, :128].astype(F32)
+        hit = (named[:, :128] == expert) | (named[:, 128:] == expert)
+        m.hot[...] = jnp.where(hit, 1.0, 0.0)
+        m.sig[...] = sig
+        top, low = halves(sig * m.hot[...])
+        m.gg[:, :128] = top
+        m.gg[:, 128:] = low
+        l_v.wait()
+        l_ev.wait()
+        l_sel.wait()
+        m.acc[mem, :] = jnp.zeros((SEG, HD), F32)
+
+        def values(cols, _):
+            top, low = halves(dot_nt(m.xn[...], wv[cols, :]) * gates_wide(m.exv, cols))
+            m.acc[mem, :] += dot(top, m.sel[cols, :HD]) + dot(low, m.sel[cols, :HD])
+        for_wide(values)
+        m.v[own, :] = m.acc[mem, :].astype(BF)
+
+        @pl.when(t < last_t)
+        def _():
+            v_copy().start()
+        l_q.wait()
+        m.q[...] = dot_nt(m.xn[...], m.wq[...]).astype(BF)
+        l_oc.wait()
+        turn(0, 0, m.oc[...])
+        turn(3, 1, m.xn[...])
+
+        @pl.when(t > 0)
+        def _():
+            k_copy().wait_recv()
+            v_copy().wait_recv()
+
+        @pl.when(t == 0)
+        def _():
+            m.k[mem, :] = jnp.zeros((SEG, HD), BF)
+            m.v[mem, :] = jnp.zeros((SEG, HD), BF)
+        m.acc[mem, :] = jnp.zeros((SEG, HD), F32)
+
+        def attend(h, _):
+            m.acc[mem, :] += dot(weights_of(h).astype(BF), head_only(m.v[...], h))
+            return 0
+        lax.fori_loop(0, H, attend, 0)
+        m.att[...] = m.acc[mem, :].astype(BF)
+        m.g_o[mem, 2176:2304] = jnp.zeros((SEG, 128), BF)
+        l_eo.wait()
+
+        def mixing(cols, _):
+            m.g_o[mem, cols] = (gates_wide(m.exo, cols) * dot_nt(m.att[...], m.sel[cols, :HD])).astype(BF)
+        for_wide(mixing)
+        go_copy().start()
+        l_wo.wait()
+        m.mid[...] = m.x[...].astype(F32) + dot(m.g_o[mem, :WIDE], wo[...])
+
+        def norm2(rows):
+            unit, _ = unit_rows(m.mid[rows, :])
+            m.hn[rows, :] = (unit * m.gains[1:2, :].astype(F32)).astype(BF)
+        for_rows(32, norm2)
+        at_copy(0, 0).wait_send()
+        turn(1, 0, m.hn[...])
+
+    pl.run_scoped(forward, pltpu.VMEM((WIDE, D), BF), pltpu.VMEM((WIDE, D), BF))
+
+    def backward(parts):
+        ex = Exchange(parts, recv, (m.ssem, m.rsem), m.stage, m.out_sem, flat_h)
+
+        def product(i, g):
+            return dot(m.at[i].reshape(512, 2 * SEG), g)
+
+        def tiles(i, g, tile):
+            acc = product(i, g)
+            for k in range(acc.shape[1] // TILE):
+                store_tile(parts, tile + k, acc[:, k * TILE:(k + 1) * TILE])
+
+        def two(i):
+            return pl.ds(pl.multiple_of(i * 2 * TILE, 2 * TILE), 2 * TILE)
+
+        m.lo[...] = m.mid[...]
+        m.nsc[...] = jnp.zeros((SEG, D), F32)
+        at_copy(0, 0).wait_recv()
+        at_copy(1, 0).wait_recv()
+
+        def block(j, _):
+            b = rem(j, 2)
+            g = rem(j, NG)
+            for cp in ff_loads(j):
+                cp.wait()
+            pre = dot(m.hn[...], m.wu[b])
+            cdf = 0.5 * (1.0 + lax.erf(pre * 0.7071067811865476))
+            pdf = jnp.exp(-0.5 * pre * pre) * 0.3989422804014327
+            up = dot_nt(m.oc[...], m.wd[b])
+
+            @pl.when(j >= NG)
+            def _():
+                for cp in ff_copies(j - NG):
+                    cp.wait_send()
+            m.act[g, mem] = (pre * cdf).astype(BF)
+            m.uc[g, mem] = (up * (cdf + pre * pdf)).astype(BF)
+            for cp in ff_copies(j):
+                cp.start()
+
+            @pl.when(j > 1)
+            def _():
+                weights_grad(j - 1)
+            m.lo[...] += dot(m.act[g, mem], m.wd[b])
+            m.nsc[...] += dot_nt(m.uc[g, mem], m.wu[b])
+
+            @pl.when(j + 2 < NFF)
+            def _():
+                for cp in ff_loads(j + 2):
+                    cp.start()
+
+            @pl.when(j == 0)
+            def _():
+                weights_grad(0)
+                ex.step1_ab(0)
+
+            @pl.when((lax.rem(j, 2) == 0) & (j > 0))
+            def _():
+                ex.tick(j // 2 - 1)
+            return 0
+
+        def weights_grad(j):
+            for cp in ff_copies(j):
+                cp.wait_recv()
+            tiles(0, m.act[rem(j, NG)], 8 * j)
+            tiles(1, m.uc[rem(j, NG)], 8 * j + 4)
+        lax.fori_loop(0, NFF, block, 0)
+        weights_grad(NFF - 1)
+        ex.tick(3)
+        for j in range(NFF - NG, NFF):
+            for cp in ff_copies(j):
+                cp.wait_send()
+        m.ob[...] = m.lo[...].astype(BF)
+        l_lo = pltpu.make_async_copy(m.ob, lo_h, m.st.at[0])
+        l_lo.start()
+
+        def norm2_back(rows):
+            unit, inv = unit_rows(m.mid[rows, :])
+            cot = m.nsc[rows, :]
+            mcot = m.oc[rows, :].astype(F32) + norm_back(unit, inv, cot * m.gains[1:2, :].astype(F32))
+            m.lo[rows, :] = mcot
+            m.bc[rows, :] = mcot.astype(BF)
+            m.hn[rows, :] = (cot * unit).astype(BF)
+        for_rows(32, norm2_back)
+        at_copy(3, 1).wait_send()
+        turn(2, 1, m.bc[...])
+        at_copy(1, 0).wait_send()
+        turn(5, 0, m.hn[...])
+        go_copy().wait_recv()
+        at_copy(2, 1).wait_recv()
+
+        def out_grad(i, _):
+            tiles(2, m.g_o[:, two(i)], 64 + 2 * i)
+            return 0
+        lax.fori_loop(0, 9, out_grad, 0)
+        ex.tick(4)
+
+        def through_output(wo):
+            load(11, wo_h, wo).wait()
+            m.acc[mem, :] = jnp.zeros((SEG, HD), F32)
+            m.ogc[...] = jnp.zeros((SEG, 128), F32)
+
+            def mixed(cols, _):
+                cot = dot_nt(m.bc[...], wo[cols, :])
+                seen = (cot * dot_nt(m.att[...], m.sel[cols, :HD])).astype(BF)
+                m.ogc[...] += dot_nt(seen, m.exo[:128, cols])
+                chosen = (cot * gates_wide(m.exo, cols)).astype(BF)
+                m.acc[mem, :] += dot(chosen, m.sel[cols, :HD])
+            for_wide(mixed)
+            m.att[...] = m.acc[mem, :].astype(BF)
+        pl.run_scoped(through_output, pltpu.VMEM((WIDE, D), BF))
+        ex.tick(5)
+
+        def values_back(h, _):
+            probs = weights_of(h)
+            cot = head_only(m.att[...], h)
+            m.acc[...] += dot_tn(probs.astype(BF), cot)
+            return 0
+
+        m.acc[...] = jnp.zeros((2 * SEG, HD), F32)
+        lax.fori_loop(0, H, values_back, 0)
+        m.vc[...] = m.acc[...].astype(BF)
+
+        @pl.when(t > 0)
+        def _():
+            vc_copy().start()
+        ex.tick(6)
+        m.acc[...] = jnp.zeros((2 * SEG, HD), F32)
+        m.qc[...] = jnp.zeros((SEG, HD), F32)
+
+        def scores_back(h, _):
+            probs = weights_of(h)
+            pc = dot_nt(head_only(m.att[...], h), m.v[...])
+            sc = (probs * (pc - jnp.sum(probs * pc, axis=-1, keepdims=True))).astype(BF)
+            m.qc[...] += dot(sc, head_only(m.k[...], h)) * scale
+            m.acc[...] += dot_tn(sc, head_only(m.q[...], h)) * scale
+            return 0
+        lax.fori_loop(0, H, scores_back, 0)
+        m.kc[...] = m.acc[...].astype(BF)
+
+        @pl.when(t > 0)
+        def _():
+            kc_copy().start()
+        m.g_p[mem, HD:512] = jnp.zeros((SEG, 512 - HD), BF)
+        m.g_p[mem, 512 + HD:1024] = jnp.zeros((SEG, 512 - HD), BF)
+        m.g_p[mem, :HD] = m.qc[...].astype(BF)
+        ex.tick(7)
+
+        @pl.when(t < last_t)
+        def _():
+            vc_copy().wait_recv()
+            kc_copy().wait_recv()
+
+        @pl.when(t == last_t)
+        def _():
+            m.kn[...] = jnp.zeros((SEG, HD), BF)
+            m.vn[...] = jnp.zeros((SEG, HD), BF)
+        m.g_p[mem, 512:512 + HD] = (m.kc[own, :].astype(F32) + m.kn[...].astype(F32)).astype(BF)
+        l_lo.wait()
+
+        own_cot, next_cot = m.mid, m.nsc
+
+        def through_values(wv, vg):
+            load(5, wv_h, wv).wait()
+            own_cot[...] = dot(m.kc[own, :], m.wk[...]) + dot(m.g_p[mem, :HD], m.wq[...])
+            next_cot[...] = dot(m.kn[...], m.wk[...])
+            vg[...] = jnp.zeros((2, SEG, 128), F32)
+
+            def values(cols, lo):
+                proj = dot_nt(m.xn[...], wv[cols, :])
+                gate = gates_wide(m.exv, cols)
+                vo = dot_nt(m.vc[own, :], m.sel[cols, :HD])
+                vn = dot_nt(m.vn[...], m.sel[cols, :HD])
+                for i, v in enumerate((vo, vn)):
+                    vg[i] += dot_nt((v * proj).astype(BF), m.exv[:128, cols])
+                po = (gate * vo).astype(BF)
+                pn = (gate * vn).astype(BF)
+                own_cot[...] += dot(po, wv[cols, :])
+                next_cot[...] += dot(pn, wv[cols, :])
+                both = (po.astype(F32) + pn.astype(F32)).astype(BF)
+                if isinstance(lo, int):
+                    m.g_p[mem, 1024 + lo:1024 + WIDE] = both
+                else:
+                    m.g_p[mem, pl.ds(pl.multiple_of(1024 + lo, WB), WB)] = both
+            for_wide(values)
+            slope = m.sig[...] * (1.0 - m.sig[...]) * m.hot[...]
+            lo_cot = ((vg[0] + m.ogc[...]) * slope).astype(BF)
+            ln_cot = (vg[1] * slope).astype(BF)
+            own_cot[...] += dot(lo_cot, m.wrp[...])
+            next_cot[...] += dot(ln_cot, m.wrp[...])
+            both = (lo_cot.astype(F32) + ln_cot.astype(F32)).astype(BF)
+            lane = lax.broadcasted_iota(jnp.int32, (SEG, 128), 1)
+            m.g_p[mem, 3200:3328] = jnp.where(lane < LOGIT, m.g_p[mem, 3200:3328], both)
+            gp_copy().start()
+
+            def norm1_back(rows):
+                unit, inv = unit_rows(m.x[rows, :].astype(F32))
+                cot = own_cot[rows, :]
+                m.lo[rows, :] += norm_back(unit, inv, cot * m.gains[0:1, :].astype(F32))
+                m.hn[rows, :] = ((cot + next_cot[rows, :]) * unit).astype(BF)
+            for_rows(32, norm1_back)
+        pl.run_scoped(through_values, pltpu.VMEM((WIDE, D), BF), pltpu.VMEM((2, SEG, 128), F32))
+        l_ig = pltpu.make_async_copy(m.lo, ig_h, m.st.at[1])
+        l_ig.start()
+        at_copy(2, 1).wait_send()
+        turn(4, 1, m.hn[...])
+        ex.tick(8)
+        gp_copy().wait_recv()
+        at_copy(3, 1).wait_recv()
+
+        def proj_grad(i, _):
+            tiles(3, m.g_p[:, two(i)], 82 + 2 * i)
+            return 0
+        lax.fori_loop(0, 12, proj_grad, 0)
+        last = product(3, m.g_p[:, 3072:3328])
+        store_tile(parts, 106, last[:, :TILE])
+        last = last[:, TILE:]
+        lane = lax.broadcasted_iota(jnp.int32, (2 * SEG, TILE), 1)
+        at_copy(5, 0).wait_recv()
+        at_copy(4, 1).wait_recv()
+        for i, at in ((4, 104), (5, 105)):
+            last += product(i, jnp.where(lane == at, 1.0, 0.0).astype(BF))
+        store_tile(parts, 107, last)
+
+        def run(i, _):
+            ex.tick(i)
+            return 0
+        lax.fori_loop(9, NS + 5, run, 0)
+        ex.finish()
+        l_ig.wait()
+
+    pl.run_scoped(backward, *P_SCRATCH)
+    at_copy(5, 0).wait_send()
+    at_copy(4, 1).wait_send()
+    go_copy().wait_send()
+    gp_copy().wait_send()
+
+    @pl.when(t < last_t)
+    def _():
+        k_copy().wait_send()
+        v_copy().wait_send()
+
+    @pl.when(t > 0)
+    def _():
+        kc_copy().wait_send()
+        vc_copy().wait_send()
+
+
+def tables():
+    col = np.arange(WIDE)
+    sel = (col // (E * DH) * DH + col % DH)[:, None] == np.arange(HD)[None, :]
+    branch = np.arange(128)[:, None]
+    exv = branch == LOGIT + col[None, :] // DH
+    exo = branch == LOGIT + H * E + col[None, :] // DH
+    exv, exo = (np.concatenate([v, v]) for v in (exv, exo))
+    sel = np.pad(sel, ((0, 0), (0, 512 - HD)))
+    exv, exo = (np.pad(v, ((0, 0), (0, 2304 - WIDE))) for v in (exv, exo))
+    lane = np.arange(128) - LOGIT
+    inside = (lane >= 0) & (lane < 2 * H * E)
+    pick = (np.arange(2 * H)[:, None] == lane[None, :] // E) & inside
+    spread = np.zeros((128, 256), np.float32)
+    spread[:2 * H, :128] = pick
+    spread[16:16 + 2 * H, 128:] = pick
+    spread[127, :128] = np.where(inside, lane % E, -1)
+    return tuple(v.astype(ml_dtypes.bfloat16) for v in (sel, exv, exo, spread))
+
+
+def fused_device(layer_input, routes, memory_lengths, norm_gains, w_query, w_key, w_value,
+                 w_router, w_output, w_up, w_down, output_cot):
+    anywhere = pl.BlockSpec(memory_space=pl.ANY)
+    specs = [anywhere] * 16
+    specs[2] = pl.BlockSpec(memory_space=pltpu.SMEM)
+    out, grad, flat = pl.pallas_call(
+        layer_kernel,
+        out_shape=(jax.ShapeDtypeStruct((SEG, D), BF), jax.ShapeDtypeStruct((SEG, D), F32),
+                   jax.ShapeDtypeStruct((32, FLAT), F32)),
+        in_specs=specs,
+        out_specs=(anywhere,) * 3,
+        scratch_shapes=layer_scratch() + RECV_SCRATCH,
+        compiler_params=pltpu.CompilerParams(
+            collective_id=0, has_side_effects=True, vmem_limit_bytes=VMEM_LIMIT),
+        name="layer",
+    )(layer_input[0], jnp.transpose(routes[0], (1, 2, 0)), memory_lengths, norm_gains, w_query.T, w_key.T, w_value.T, w_router.T,
+      w_output, w_up, w_down, output_cot[0], *tables())
+    shapes = ((SEG, D), BF), ((SEG, D), F32), ((2, 32), F32), ((32, HD), F32), ((32, HD), F32), \
+        ((32, WIDE), F32), ((32, 2 * H * E), F32), ((32, WIDE), F32), ((32, FF), F32), ((32, FF), F32)
+    vm = pl.BlockSpec(memory_space=pltpu.VMEM)
+    res = pl.pallas_call(
+        split_kernel,
+        out_shape=tuple(jax.ShapeDtypeStruct(*v) for v in shapes),
+        in_specs=(anywhere, anywhere, anywhere),
+        out_specs=(vm,) * 10,
+        scratch_shapes=[pltpu.VMEM((32, FLAT), F32), pltpu.SemaphoreType.DMA((3,))],
+        compiler_params=pltpu.CompilerParams(vmem_limit_bytes=VMEM_LIMIT),
+        name="split",
+    )(out, grad, flat)
+    return (res[0][None], res[1][None], *res[2:7], res[7].T, res[8], res[9].T)
+
+
+def split_kernel(out_h, grad_h, flat_h, lo, ig, gains, dq, dk, dv, dr, do, du, dd, flat, sem):
+    copies = [pltpu.make_async_copy(flat_h, flat, sem.at[2]), pltpu.make_async_copy(out_h, lo, sem.at[0]),
+              pltpu.make_async_copy(grad_h, ig, sem.at[1])]
+    for cp in copies:
+        cp.start()
+    copies.pop(0).wait()
+    for j in range(NFF):
+        dd[:, j * FFB:(j + 1) * FFB] = flat[:, 2 * j * FFB:(2 * j + 1) * FFB]
+        du[:, j * FFB:(j + 1) * FFB] = flat[:, (2 * j + 1) * FFB:(2 * j + 2) * FFB]
+    do[...] = flat[:, 2 * FF:2 * FF + WIDE]
+    base = 82 * TILE
+    dq[...] = flat[:, base:base + HD]
+    dk[...] = flat[:, base + 512:base + 512 + HD]
+    dv[...] = flat[:, base + 1024:base + 1024 + WIDE]
+    tail = flat[:, 107 * TILE:108 * TILE]
+    dr[...] = tail[:, LOGIT:LOGIT + 2 * H * E]
+    gains[...] = jnp.transpose(tail)[104:106, :]
+    for cp in copies:
+        cp.wait()
+
+
 def solution(mesh):
     placed = (
         P("seq", "tm", None),
@@ -259,8 +1156,9 @@
         P(),
         P("seq", "tm", None),
     )
+    fused = mesh.shape["seq"] == 2 and mesh.shape["tm"] == 16
     return jax.shard_map(
-        per_device,
+        fused_device if fused else per_device,
         mesh=mesh,
         in_specs=placed,
         out_specs=(

time: 1320 us -> 167 us (0.13)
  waiting for transfers between devices: 1140 us -> 0 us
  Pallas kernels: 0 us -> 165 us
  matrix products: 114 us -> 0 us
  between operations: 16.2 us -> 1.46 us
  local copies, waits for them, and re-layouts: 13.9 us -> 0 us
  other arithmetic: 13.4 us -> 0 us
    reduce_scatter x7 -> x0, waiting for transfers between devices: 1060 us -> none  [the longest x1 188 us: per_device(): lax.psum_scatter(grad_down, ('seq', 'tm'), scatter_dimension=1, tiled=True)]
    pallas_call x0 -> x2, Pallas kernels: none -> 165 us  [the longest x1 162 us: fused_device(): pl.pallas_call(layer_kernel, out_shape=(jax.ShapeDtypeStruct((SEG, D), BF...]
    dot_general x45 -> x0, matrix products: 114 us -> none  [the longest x15 44.9 us: tr_times(): lax.dot_general(left_op, right_op, (((0,), (0,)), ((), ())), preferred_el...]
    unnamed x9 -> x0, waiting for transfers between devices: 85.9 us -> none
  transfers between devices with their start and end apart: 12 -> 0, of which waited for: 8 -> 0; matrix products, arithmetic and copies ran while one was open for 6% -> 0% of each run, Pallas kernels for 0% -> 0%
where the time goes in v1:
time: 167 us
  Pallas kernels  165 us (99%)
    pallas_call x1, Pallas kernels, fused_device(): pl.pallas_call(layer_kernel, out_shape=(jax.ShapeDtypeStruct((SEG, D), BF...  162 us
    pallas_call x1, Pallas kernels, fused_device(): pl.pallas_call(split_kernel, out_shape=tuple((jax.ShapeDtypeStruct(*v) fo...  3.68 us

profile of v1, /device:TPU:0, one launch (start us, length us, event | category | flops | bytes accessed | tf_op | source)
XLA Modules:
  0.0 166.8 jit_solution(4888444089036636086)
XLA Ops:
  1.3 161.6 %layer.1 = (bf16[256,1024]{1,0:T(8,128)(2,1)}, f32[256,1024]{1,0:T(8,128)}, f32[32,13824]{1,0:T(8,128)}) custom-call(bf16[256,1024]{1,0:T(8,128)(2,1)} %bitcast.16, s32[8,2,256]{2,1,0:T(2,128)} %bitcast.19, s32[1,1]{1,0:T(1,128)S(6)} %copy.26.len_s, bf16[2,1024]{1,0:T(2,128)(2,1)} %gains_h.1, bf16[448,1024]{1,0:T(8,128)(2,1)} %bitcast.14, ...), custom_call_target="tpu_custom_call" | custom-call | tf_op jit(solution)/shard_map/layer/pallas_call | solution.py:1096
  162.9 3.7 %split.1 = (bf16[256,1024]{1,0:T(8,128)(2,1)}, f32[256,1024]{1,0:T(8,128)}, f32[2,32]{1,0:T(2,128)}, f32[32,448]{1,0:T(8,128)}, f32[32,448]{1,0:T(8,128)}, /*ind...) custom-call(bf16[256,1024]{1,0:T(8,128)(2,1)} %get-tuple-element.23.out_h, ...), custom_call_target="tpu_custom_call" | custom-call | tf_op jit(solution)/shard_map/split/pallas_call | solution.py:1111

commit v2 on v1

--- a/solution.py
+++ b/solution.py
@@ -253,23 +253,28 @@
 VMEM_LIMIT = 64 << 20
 
 MESH_ID = pl.DeviceIdType.MESH
-NS = 12
 TILE = 128
-AB_T = 7
-C_T = 2
-PER = AB_T + C_T
-AB_W = AB_T * TILE
-C_W = C_T * TILE
-FLAT = NS * PER * TILE
+PIECES = [(6, 2)] * 2 + [(7, 2)] * 8 + [(5, 2), (4, 1), (3, 1), (2, 0), (2, 0)]
+NS = len(PIECES)
+TILES = sum(a + b for a, b in PIECES)
+FLAT = TILES * TILE
+MOST_FIRST = max(a for a, _ in PIECES) * TILE
+MOST_LAST = max(b for _, b in PIECES) * TILE
+MOST = max(a + b for a, b in PIECES) * TILE
+N1 = 6
 NR = 4
-NZ = 6
-FIRST = slice(0, AB_W)
-LAST = slice(AB_W, AB_W + C_W)
+NZ = 7
 HALF = (slice(0, 16), slice(16, 32))
 
 
-def rem(a, n):
-    return a % n if isinstance(a, int) else lax.rem(a, n)
+class Piece:
+    def __init__(self, p):
+        start = sum(a + b for a, b in PIECES[:p]) * TILE
+        self.p, self.f, self.r, self.q = p, p % N1, p % NR, p % NZ
+        self.wf, self.wl = (v * TILE for v in PIECES[p])
+        self.first = slice(start, start + self.wf)
+        self.last = slice(start + self.wf, start + self.wf + self.wl)
+        self.all = slice(start, start + self.wf + self.wl)
 
 
 def place():
@@ -278,12 +283,15 @@
     return s, t, t // 4, (t // 2) % 2, t % 2
 
 
+def rem(a, n):
+    return a % n if isinstance(a, int) else lax.rem(a, n)
+
+
 def store_tile(parts, tile, value):
-    piece = tile // PER
-    slot = tile - piece * PER
-    at = slot * TILE
-    cols = slice(at, at + TILE) if isinstance(at, int) else pl.ds(pl.multiple_of(at, TILE), TILE)
-    parts[piece, :, :, :, :, cols] = value.reshape(2, 4, 2, 32, TILE).astype(jnp.bfloat16)
+    at = tile * TILE
+    width = value.shape[1]
+    cols = slice(at, at + width) if isinstance(at, int) else pl.ds(pl.multiple_of(at, TILE), width)
+    parts[:, :, :, :, cols] = value.reshape(2, 4, 2, 32, width).astype(jnp.bfloat16)
 
 
 class Exchange:
@@ -299,127 +307,129 @@
         self.to_up = {"seq": s, "tm": t + 4}
         self.to_down = {"seq": s, "tm": t - 4}
 
-    def copy(self, kind, piece, src, dst, dev):
+    def copy(self, kind, g, src, dst, dev):
         return pltpu.make_async_remote_copy(
-            src_ref=src, dst_ref=dst, send_sem=self.ssem.at[kind, piece],
-            recv_sem=self.rsem.at[kind, piece], device_id=dev, device_id_type=MESH_ID)
-
-    def c_xa(self, p):
-        return self.copy(0, p, self.parts.at[p, 1 - self.s, :, :, HALF[0], FIRST], self.xa.at[rem(p, NR)], self.to_x)
-
-    def c_yb(self, p):
-        return self.copy(1, p, self.parts.at[p, :, :, 1 - self.y, HALF[1], FIRST], self.yb.at[rem(p, NR)], self.to_y)
-
-    def c_ya(self, p):
-        return self.copy(2, p, self.parts.at[p, self.s, :, 1 - self.y, HALF[0], FIRST], self.ya.at[rem(p, NR)], self.to_y)
-
-    def c_xb(self, p):
-        return self.copy(3, p, self.parts.at[p, 1 - self.s, :, self.y, HALF[1], FIRST], self.xb.at[rem(p, NR)], self.to_x)
-
-    def c_xc(self, p):
-        return self.copy(4, p, self.parts.at[p, 1 - self.s, self.z, :, :, LAST], self.xc.at[rem(p, NR)], self.to_x)
-
-    def c_yc(self, p):
-        return self.copy(5, p, self.parts.at[p, self.s, self.z, 1 - self.y, :, LAST], self.yc.at[rem(p, NR)], self.to_y)
-
-    def c_up(self, p, z):
-        return self.copy(6, p, self.parts.at[p, self.s, z + 1:4, self.y, :, FIRST], self.zu.at[rem(p, NZ), z:3], self.to_up)
-
-    def c_down(self, p, z):
-        return self.copy(7, p, self.parts.at[p, self.s, 0:z, self.y, :, FIRST], self.zd.at[rem(p, NZ), 0:z], self.to_down)
-
-    def c_upc(self, p, z):
-        return self.copy(8, p, self.parts.at[p, :, z + 1:4, :, :, LAST], self.zuc.at[rem(p, NZ), :, z:3], self.to_up)
-
-    def c_downc(self, p, z):
-        return self.copy(9, p, self.parts.at[p, :, 0:z, :, :, LAST], self.zdc.at[rem(p, NZ), :, 0:z], self.to_down)
-
-    def z_step(self, p, k, is_c):
+            src_ref=src, dst_ref=dst, send_sem=self.ssem.at[kind, g.p],
+            recv_sem=self.rsem.at[kind, g.p], device_id=dev, device_id_type=MESH_ID)
+
+    def c_xa(self, g):
+        return self.copy(0, g, self.parts.at[1 - self.s, :, :, HALF[0], g.first], self.xa.at[g.f, :, :, :, :g.wf], self.to_x)
+
+    def c_yb(self, g):
+        return self.copy(1, g, self.parts.at[:, :, 1 - self.y, HALF[1], g.first], self.yb.at[g.f, :, :, :, :g.wf], self.to_y)
+
+    def c_ya(self, g):
+        return self.copy(2, g, self.parts.at[self.s, :, 1 - self.y, HALF[0], g.first], self.ya.at[g.r, :, :, :g.wf], self.to_y)
+
+    def c_xb(self, g):
+        return self.copy(3, g, self.parts.at[1 - self.s, :, self.y, HALF[1], g.first], self.xb.at[g.r, :, :, :g.wf], self.to_x)
+
+    def c_xc(self, g):
+        return self.copy(4, g, self.parts.at[1 - self.s, self.z, :, :, g.last], self.xc.at[g.r, :, :, :g.wl], self.to_x)
+
+    def c_yc(self, g):
+        return self.copy(5, g, self.parts.at[self.s, self.z, 1 - self.y, :, g.last], self.yc.at[g.r, :, :g.wl], self.to_y)
+
+    def c_up(self, g, z):
+        return self.copy(6, g, self.parts.at[self.s, z + 1:4, self.y, :, g.first], self.zu.at[g.q, z:3, :, :g.wf], self.to_up)
+
+    def c_down(self, g, z):
+        return self.copy(7, g, self.parts.at[self.s, 0:z, self.y, :, g.first], self.zd.at[g.q, 0:z, :, :g.wf], self.to_down)
+
+    def c_upc(self, g, z):
+        return self.copy(8, g, self.parts.at[:, z + 1:4, :, :, g.last], self.zuc.at[g.q, :, z:3, :, :, :g.wl], self.to_up)
+
+    def c_downc(self, g, z):
+        return self.copy(9, g, self.parts.at[:, 0:z, :, :, g.last], self.zdc.at[g.q, :, 0:z, :, :, :g.wl], self.to_down)
+
+    def add(self, at, cols, value):
+        self.parts[(*at, cols)] = self.parts[(*at, cols)] + value
+
+    def z_step(self, g, k, is_c):
+        if is_c and not g.wl:
+            return
         up, down = (self.c_upc, self.c_downc) if is_c else (self.c_up, self.c_down)
+        rows = slice(None)
 
         def add(u, src, at):
             if is_c:
                 def body(i, _):
                     a, b = i // 2, i % 2
-                    self.parts[p, a, u, b, :, LAST] = self.parts[p, a, u, b, :, LAST] + src[rem(p, NZ), a, at, b]
+                    self.add((a, u, b, rows), g.last, src[g.q, a, at, b, :, :g.wl])
                     return 0
                 lax.fori_loop(0, 4, body, 0)
             else:
-                self.parts[p, self.s, u, self.y, :, FIRST] = self.parts[p, self.s, u, self.y, :, FIRST] + src[rem(p, NZ), at]
+                self.add((self.s, u, self.y, rows), g.first, src[g.q, at, :, :g.wf])
 
         @pl.when(self.z == k - 1)
         def _():
             z = k - 1
             if z > 0:
-                up(p, z - 1).wait_recv()
+                up(g, z - 1).wait_recv()
                 for u in range(z + 1, 4):
                     add(u, self.zuc if is_c else self.zu, u - 1)
             if z < 3:
-                up(p, z).start()
+                up(g, z).start()
 
         @pl.when(self.z == 4 - k)
         def _():
             z = 4 - k
             if z < 3:
-                down(p, z + 1).wait_recv()
+                down(g, z + 1).wait_recv()
                 for u in range(0, z):
                     add(u, self.zdc if is_c else self.zd, u)
             if z > 0:
-                down(p, z).start()
-
-    def step1_ab(self, p):
-        self.c_xa(p).start()
-        self.c_yb(p).start()
-
-    def step1(self, p):
-        if isinstance(p, int):
-            if p > 0:
-                self.step1_ab(p)
-        else:
-            pl.when(p > 0)(lambda: self.step1_ab(p))
-        self.z_step(p, 1, True)
-
-    def step2(self, p):
-        self.c_xa(p).wait_recv()
+                down(g, z).start()
+
+    def step1(self, g):
+        self.c_xa(g).start()
+        self.c_yb(g).start()
+        self.z_step(g, 1, True)
+
+    def step2(self, g):
+        self.c_xa(g).wait_recv()
 
         def body(i, _):
             a, b = i // 2, i % 2
-            self.parts[p, self.s, a, b, HALF[0], FIRST] = self.parts[p, self.s, a, b, HALF[0], FIRST] + self.xa[rem(p, NR), a, b]
+            self.add((self.s, a, b, HALF[0]), g.first, self.xa[g.f, a, b, :, :g.wf])
             return 0
         lax.fori_loop(0, 8, body, 0)
-        self.c_ya(p).start()
-        self.c_yb(p).wait_recv()
+        self.c_ya(g).start()
+        self.c_yb(g).wait_recv()
 
         def body(i, _):
             a, b = i // 4, i % 4
-            self.parts[p, a, b, self.y, HALF[1], FIRST] = self.parts[p, a, b, self.y, HALF[1], FIRST] + self.yb[rem(p, NR), a, b]
+            self.add((a, b, self.y, HALF[1]), g.first, self.yb[g.f, a, b, :, :g.wf])
             return 0
         lax.fori_loop(0, 8, body, 0)
-        self.c_xb(p).start()
-        self.z_step(p, 2, True)
-
-    def step3(self, p):
-        self.c_ya(p).wait_recv()
-        self.c_xb(p).wait_recv()
+        self.c_xb(g).start()
+        self.z_step(g, 2, True)
+
+    def step3(self, g):
+        self.c_ya(g).wait_recv()
+        self.c_xb(g).wait_recv()
 
         def body(b, _):
-            self.parts[p, self.s, b, self.y, HALF[0], FIRST] = self.parts[p, self.s, b, self.y, HALF[0], FIRST] + self.ya[rem(p, NR), b]
-            self.parts[p, self.s, b, self.y, HALF[1], FIRST] = self.parts[p, self.s, b, self.y, HALF[1], FIRST] + self.xb[rem(p, NR), b]
+            self.add((self.s, b, self.y, HALF[0]), g.first, self.ya[g.r, b, :, :g.wf])
+            self.add((self.s, b, self.y, HALF[1]), g.first, self.xb[g.r, b, :, :g.wf])
             return 0
         lax.fori_loop(0, 4, body, 0)
-        self.z_step(p, 1, False)
-        self.z_step(p, 3, True)
-
-    def step4(self, p):
-        self.z_step(p, 2, False)
-        self.z_step(p, 4, True)
+        self.z_step(g, 1, False)
+        self.z_step(g, 3, True)
+
+    def step4(self, g):
+        self.z_step(g, 2, False)
+        if not g.wl:
+            return
+        self.z_step(g, 4, True)
         z = self.z
+        rows = slice(None)
 
         @pl.when(z > 0)
         def _():
             def body(i, _):
                 a, b = i // 2, i % 2
-                self.parts[p, a, z, b, :, LAST] = self.parts[p, a, z, b, :, LAST] + self.zuc[rem(p, NZ), a, z - 1, b]
+                self.add((a, z, b, rows), g.last, self.zuc[g.q, a, z - 1, b, :, :g.wl])
                 return 0
             lax.fori_loop(0, 4, body, 0)
 
@@ -427,98 +437,100 @@
         def _():
             def body(i, _):
                 a, b = i // 2, i % 2
-                self.parts[p, a, z, b, :, LAST] = self.parts[p, a, z, b, :, LAST] + self.zdc[rem(p, NZ), a, z, b]
+                self.add((a, z, b, rows), g.last, self.zdc[g.q, a, z, b, :, :g.wl])
                 return 0
             lax.fori_loop(0, 4, body, 0)
-        self.c_xc(p).start()
-
-    def step5(self, p):
-        self.z_step(p, 3, False)
-        self.c_xc(p).wait_recv()
+        self.c_xc(g).start()
+
+    def step5(self, g):
+        self.z_step(g, 3, False)
+        if not g.wl:
+            return
+        self.c_xc(g).wait_recv()
         for b in range(2):
-            self.parts[p, self.s, self.z, b, :, LAST] = self.parts[p, self.s, self.z, b, :, LAST] + self.xc[rem(p, NR), b]
-        self.c_yc(p).start()
-
-    def step6(self, p):
-        self.z_step(p, 4, False)
+            self.add((self.s, self.z, b, slice(None)), g.last, self.xc[g.r, b, :, :g.wl])
+        self.c_yc(g).start()
+
+    def step6(self, g):
+        self.z_step(g, 4, False)
         z = self.z
-        k = p % 2
-
-        @pl.when(p >= 2)
-        def _():
-            self.c_out(p - 2).wait()
-        cols, colc = slice(0, AB_W), slice(AB_W, AB_W + C_W)
-        mine = self.parts[p, self.s, z, self.y, :, FIRST].astype(jnp.float32)
+        k = g.p % 2
+        if g.p >= 2:
+            self.c_out(Piece(g.p - 2)).wait()
+        mine = self.parts[self.s, z, self.y, :, g.first].astype(jnp.float32)
 
         @pl.when(z == 0)
         def _():
-            self.stage[k, :, cols] = mine + self.zd[rem(p, NZ), 0].astype(jnp.float32)
+            self.stage[k, :, :g.wf] = mine + self.zd[g.q, 0, :, :g.wf].astype(jnp.float32)
 
         @pl.when(z == 3)
         def _():
-            self.stage[k, :, cols] = mine + self.zu[rem(p, NZ), 2].astype(jnp.float32)
+            self.stage[k, :, :g.wf] = mine + self.zu[g.q, 2, :, :g.wf].astype(jnp.float32)
 
         @pl.when((z > 0) & (z < 3))
         def _():
-            self.stage[k, :, cols] = (mine + self.zu[rem(p, NZ), z - 1].astype(jnp.float32)) + self.zd[rem(p, NZ), z].astype(jnp.float32)
-        self.c_yc(p).wait_recv()
-        self.stage[k, :, colc] = self.parts[p, self.s, z, self.y, :, LAST].astype(jnp.float32) + self.yc[rem(p, NR)].astype(jnp.float32)
-        self.c_out(p).start()
-
-    def c_out(self, p):
-        cols = pl.ds(pl.multiple_of(p * (PER * TILE), TILE), PER * TILE)
-        return pltpu.make_async_copy(self.stage.at[p % 2], self.out.at[:, cols], self.out_sem.at[p % 2])
+            self.stage[k, :, :g.wf] = ((mine + self.zu[g.q, z - 1, :, :g.wf].astype(jnp.float32))
+                                       + self.zd[g.q, z, :, :g.wf].astype(jnp.float32))
+        if g.wl:
+            self.c_yc(g).wait_recv()
+            self.stage[k, :, g.wf:g.wf + g.wl] = (self.parts[self.s, z, self.y, :, g.last].astype(jnp.float32)
+                                                  + self.yc[g.r, :, :g.wl].astype(jnp.float32))
+        self.c_out(g).start()
+
+    def c_out(self, g):
+        k = g.p % 2
+        return pltpu.make_async_copy(self.stage.at[k, :, :g.wf + g.wl], self.out.at[:, g.all], self.out_sem.at[k])
 
     def tick(self, t):
-        steps = (self.step1, self.step2, self.step3, self.step4, self.step5, self.step6)
+        steps = (self.step2, self.step3, self.step4, self.step5, self.step6)
         for k, step in enumerate(steps):
-            p = t - k
-            if isinstance(t, int):
-                if 0 <= p < NS:
-                    step(p)
-            else:
-                @pl.when((p >= 0) & (p < NS))
-                def _(step=step, p=p):
-                    step(p)
+            if 0 <= t - 1 - k < NS:
+                step(Piece(t - 1 - k))
+
+    def begin(self, p):
+        if p < NS:
+            self.step1(Piece(p))
 
     def finish(self):
-        self.c_out(NS - 2).wait()
-        self.c_out(NS - 1).wait()
-
-        def body(p, _):
-            self.c_xa(p).wait_send()
-            self.c_yb(p).wait_send()
-            self.c_ya(p).wait_send()
-            self.c_xb(p).wait_send()
-            self.c_xc(p).wait_send()
-            self.c_yc(p).wait_send()
-            for z in range(4):
-                @pl.when(self.z == z)
-                def _(z=z):
+        self.c_out(Piece(NS - 2)).wait()
+        self.c_out(Piece(NS - 1)).wait()
+        for p in range(NS):
+            g = Piece(p)
+            self.c_xa(g).wait_send()
+            self.c_yb(g).wait_send()
+            self.c_ya(g).wait_send()
+            self.c_xb(g).wait_send()
+            if g.wl:
+                self.c_xc(g).wait_send()
+                self.c_yc(g).wait_send()
+        for z in range(4):
+            @pl.when(self.z == z)
+            def _(z=z):
+                for p in range(NS):
+                    g = Piece(p)
                     if z < 3:
-                        self.c_up(p, z).wait_send()
-                        self.c_upc(p, z).wait_send()
+                        self.c_up(g, z).wait_send()
+                        if g.wl:
+                            self.c_upc(g, z).wait_send()
                     if z > 0:
-                        self.c_down(p, z).wait_send()
-                        self.c_downc(p, z).wait_send()
-            return 0
-        lax.fori_loop(0, NS, body, 0)
-
-
-P_SCRATCH = [pltpu.VMEM((NS, 2, 4, 2, 32, PER * TILE), jnp.bfloat16)]
+                        self.c_down(g, z).wait_send()
+                        if g.wl:
+                            self.c_downc(g, z).wait_send()
+
+
+P_SCRATCH = [pltpu.VMEM((2, 4, 2, 32, FLAT), jnp.bfloat16)]
 RECV_SCRATCH = [
-    pltpu.VMEM((NR, 4, 2, 16, AB_W), jnp.bfloat16),
-    pltpu.VMEM((NR, 2, 4, 16, AB_W), jnp.bfloat16),
-    pltpu.VMEM((NR, 4, 16, AB_W), jnp.bfloat16),
-    pltpu.VMEM((NR, 4, 16, AB_W), jnp.bfloat16),
-    pltpu.VMEM((NZ, 3, 32, AB_W), jnp.bfloat16),
-    pltpu.VMEM((NZ, 3, 32, AB_W), jnp.bfloat16),
-    pltpu.VMEM((NZ, 2, 3, 2, 32, C_W), jnp.bfloat16),
-    pltpu.VMEM((NZ, 2, 3, 2, 32, C_W), jnp.bfloat16),
-    pltpu.VMEM((NR, 2, 32, C_W), jnp.bfloat16),
-    pltpu.VMEM((NR, 32, C_W), jnp.bfloat16),
+    pltpu.VMEM((N1, 4, 2, 16, MOST_FIRST), jnp.bfloat16),
+    pltpu.VMEM((N1, 2, 4, 16, MOST_FIRST), jnp.bfloat16),
+    pltpu.VMEM((NR, 4, 16, MOST_FIRST), jnp.bfloat16),
+    pltpu.VMEM((NR, 4, 16, MOST_FIRST), jnp.bfloat16),
+    pltpu.VMEM((NZ, 3, 32, MOST_FIRST), jnp.bfloat16),
+    pltpu.VMEM((NZ, 3, 32, MOST_FIRST), jnp.bfloat16),
+    pltpu.VMEM((NZ, 2, 3, 2, 32, MOST_LAST), jnp.bfloat16),
+    pltpu.VMEM((NZ, 2, 3, 2, 32, MOST_LAST), jnp.bfloat16),
+    pltpu.VMEM((NR, 2, 32, MOST_LAST), jnp.bfloat16),
+    pltpu.VMEM((NR, 32, MOST_LAST), jnp.bfloat16),
 ]
-
 
 def greet():
     s, t, z, y, c = place()
@@ -554,7 +566,6 @@
 FFB = 512
 NFF = FF // FFB
 NG = 4
-WB = 512
 LOGIT = 64
 OWN_SIB = 24
 F32 = jnp.float32
@@ -597,22 +608,16 @@
     lax.fori_loop(0, SEG // step, inner, 0)
 
 
-def for_wide(body):
-    whole = WIDE // WB
-
-    def inner(i, _):
-        body(pl.ds(pl.multiple_of(i * WB, WB), WB), i * WB)
-        return 0
-    lax.fori_loop(0, whole, inner, 0)
-    body(slice(whole * WB, WIDE), whole * WB)
+def side_by_side(blocks):
+    return jnp.concatenate(blocks, axis=1)
 
 
 NAMES = (
-    "x", "oc", "gains", "rt", "rf", "spread", "hot", "wq", "wk", "wr", "wrp", "wu", "wd", "sel", "exv", "exo",
+    "x", "oc", "gains", "rt", "rf", "spread", "hot", "wq", "wk", "wr", "wrp", "wu", "wd", "exv", "exo",
     "xn", "hn", "mid", "lo", "nsc", "q", "k", "v", "sig", "att", "acc", "g_o", "g_p",
-    "act", "uc", "bc", "kc", "vc", "kn", "vn", "ob", "gg", "ogc", "qc",
+    "act", "uc", "bc", "kc", "vc", "kn", "vn", "ob", "gg", "ogc", "qc", "vg", "ac", "acc2",
     "at", "full",
-    "ld", "ld2", "kv_s", "kv_r", "sib_s", "sib_r", "st", "stage", "out_sem", "ssem", "rsem",
+    "ld", "ld2", "lde", "kv_s", "kv_r", "sib_s", "sib_r", "st", "stage", "out_sem", "ssem", "rsem",
 )
 
 
@@ -623,20 +628,21 @@
         v((SEG, D), BF), v((SEG, D), BF), v((2, D), BF), v((2 * H, 2, SEG), jnp.int32), v((128, SEG), BF),
         v((128, 256), BF), v((SEG, 128), F32),
         v((HD, D), BF), v((HD, D), BF), v((2 * H * E, D), BF), v((128, D), BF),
-        v((2, D, FFB), BF), v((2, FFB, D), BF), v((WIDE, 512), BF), v((256, 2304), BF), v((256, 2304), BF),
+        v((2, D, FFB), BF), v((2, FFB, D), BF), v((E, 256, HD), BF), v((E, 256, HD), BF),
         v((SEG, D), BF), v((SEG, D), BF), v((SEG, D), F32), v((SEG, D), F32), v((SEG, D), F32),
         v((SEG, HD), BF), v((2 * SEG, HD), BF), v((2 * SEG, HD), BF), v((SEG, 128), F32),
         v((SEG, HD), BF), v((2 * SEG, HD), F32), v((2 * SEG, 2304), BF), v((2 * SEG, 3328), BF),
         v((NG, 2 * SEG, FFB), BF), v((NG, 2 * SEG, FFB), BF), v((SEG, D), BF),
-        v((2 * SEG, HD), BF), v((2 * SEG, HD), BF), v((SEG, HD), BF), v((SEG, HD), BF), v((SEG, D), BF), v((SEG, 256), BF), v((SEG, 128), F32), v((SEG, HD), F32),
+        v((2 * SEG, HD), BF), v((2 * SEG, HD), BF), v((SEG, HD), BF), v((SEG, HD), BF), v((SEG, D), BF), v((SEG, 256), BF), v((SEG, 128), F32), v((SEG, HD), F32), v((2, SEG, 128), F32),
+        v((SEG, HD), BF), v((2 * SEG, HD), F32),
         v((6, 16, 32, 2 * SEG), BF), v((2, 16, 2, 32, SEG), BF),
-        dma((16,)), dma((4,)), dma((4,)), dma((4,)), dma((OWN_SIB,)), dma((OWN_SIB,)), dma((2,)),
-        v((2, 32, PER * TILE), F32), dma((2,)), dma((10, NS)), dma((10, NS)),
+        dma((16,)), dma((4,)), dma((2, 2 * E)), dma((4,)), dma((4,)), dma((OWN_SIB,)), dma((OWN_SIB,)), dma((2,)),
+        v((2, 32, MOST), F32), dma((2,)), dma((10, NS)), dma((10, NS)),
     ]
 
 
 def layer_kernel(x_h, rt_h, len_s, gains_h, wq_h, wk_h, wv_h, wr_h, wo_h, wu_h, wd_h, oc_h,
-                 sel_h, exv_h, exo_h, spread_h, lo_h, ig_h, flat_h, *scratch):
+                 exv_h, exo_h, spread_h, lo_h, ig_h, flat_h, *scratch):
     m = types.SimpleNamespace(**dict(zip(NAMES, scratch[:len(NAMES)])))
     recv = scratch[len(NAMES):]
     s, t, z, y, c = place()
@@ -706,8 +712,15 @@
     def head_only(v, h):
         return jnp.where(head_lanes(v.shape[0], h), v, jnp.zeros_like(v))
 
-    def gates_wide(table, cols):
-        return dot(m.gg[...], table[:, cols])
+    def gates_wide(table, e):
+        return dot(m.gg[...], table[e])
+
+    def expert_loads(which, n, e, src, dst):
+        return [pltpu.make_async_copy(src.at[pl.ds((h * E + e) * DH, DH)], dst.at[pl.ds(h * DH, DH)], m.lde.at[which, n])
+                for h in range(H)]
+
+    def ring(n):
+        return expert_loads(0, n, n % E, wo_h if n < E else wv_h, m.wd.at[n % 2])
 
     def weights_of(h):
         scores = dot_nt(head_only(m.q[...], h), m.k[...]) * scale
@@ -727,9 +740,11 @@
     l_sp = load(12, spread_h, m.spread)
 
     def forward(wv, wo):
-        l_v = load(5, wv_h, wv)
         l_ev = load(6, exv_h, m.exv)
-        l_sel = load(7, sel_h, m.sel)
+        l_v = [expert_loads(0, e, e, wv_h, wv.at[e]) for e in range(E)]
+        for group in l_v:
+            for cp in group:
+                cp.start()
         l_x.wait()
         l_g.wait()
 
@@ -742,7 +757,10 @@
         l_q = load(8, wq_h, m.wq)
         l_oc = load(9, oc_h, m.oc)
         l_eo = load(10, exo_h, m.exo)
-        l_wo = load(11, wo_h, wo)
+        l_wo = [expert_loads(1, e, e, wo_h, wo.at[e]) for e in range(E)]
+        for group in l_wo:
+            for cp in group:
+                cp.start()
         for j in range(2):
             for cp in ff_loads(j):
                 cp.start()
@@ -768,16 +786,13 @@
         top, low = halves(sig * m.hot[...])
         m.gg[:, :128] = top
         m.gg[:, 128:] = low
-        l_v.wait()
         l_ev.wait()
-        l_sel.wait()
-        m.acc[mem, :] = jnp.zeros((SEG, HD), F32)
-
-        def values(cols, _):
-            top, low = halves(dot_nt(m.xn[...], wv[cols, :]) * gates_wide(m.exv, cols))
-            m.acc[mem, :] += dot(top, m.sel[cols, :HD]) + dot(low, m.sel[cols, :HD])
-        for_wide(values)
-        m.v[own, :] = m.acc[mem, :].astype(BF)
+        total = jnp.zeros((SEG, HD), F32)
+        for e in range(E):
+            for cp in l_v[e]:
+                cp.wait()
+            total = total + dot_nt(m.xn[...], wv[e]) * gates_wide(m.exv, e)
+        m.v[own, :] = total.astype(BF)
 
         @pl.when(t < last_t)
         def _():
@@ -791,28 +806,34 @@
         @pl.when(t > 0)
         def _():
             k_copy().wait_recv()
-            v_copy().wait_recv()
 
         @pl.when(t == 0)
         def _():
             m.k[mem, :] = jnp.zeros((SEG, HD), BF)
             m.v[mem, :] = jnp.zeros((SEG, HD), BF)
-        m.acc[mem, :] = jnp.zeros((SEG, HD), F32)
-
-        def attend(h, _):
-            m.acc[mem, :] += dot(weights_of(h).astype(BF), head_only(m.v[...], h))
-            return 0
-        lax.fori_loop(0, H, attend, 0)
-        m.att[...] = m.acc[mem, :].astype(BF)
+        for h in range(H):
+            m.act[h, mem] = weights_of(h).astype(BF)
+
+        @pl.when(t > 0)
+        def _():
+            v_copy().wait_recv()
+        total = jnp.zeros((SEG, HD), F32)
+        for h in range(H):
+            total = total + dot(m.act[h, mem], head_only(m.v[...], h))
+        m.att[...] = total.astype(BF)
+        l_eo.wait()
         m.g_o[mem, 2176:2304] = jnp.zeros((SEG, 128), BF)
-        l_eo.wait()
-
-        def mixing(cols, _):
-            m.g_o[mem, cols] = (gates_wide(m.exo, cols) * dot_nt(m.att[...], m.sel[cols, :HD])).astype(BF)
-        for_wide(mixing)
+        total = m.x[...].astype(F32)
+        blocks = []
+        for e in range(E):
+            blocks.append((gates_wide(m.exo, e) * m.att[...].astype(F32)).astype(BF))
+            for cp in l_wo[e]:
+                cp.wait()
+            total = total + dot(blocks[e], wo[e])
+        m.mid[...] = total
+        for e in range(0, E, 2):
+            m.g_o[mem, e * HD:min(e + 2, E) * HD] = side_by_side(blocks[e:e + 2])
         go_copy().start()
-        l_wo.wait()
-        m.mid[...] = m.x[...].astype(F32) + dot(m.g_o[mem, :WIDE], wo[...])
 
         def norm2(rows):
             unit, _ = unit_rows(m.mid[rows, :])
@@ -821,7 +842,7 @@
         at_copy(0, 0).wait_send()
         turn(1, 0, m.hn[...])
 
-    pl.run_scoped(forward, pltpu.VMEM((WIDE, D), BF), pltpu.VMEM((WIDE, D), BF))
+    pl.run_scoped(forward, pltpu.VMEM((E, HD, D), BF), pltpu.VMEM((E, HD, D), BF))
 
     def backward(parts):
         ex = Exchange(parts, recv, (m.ssem, m.rsem), m.stage, m.out_sem, flat_h)
@@ -830,9 +851,7 @@
             return dot(m.at[i].reshape(512, 2 * SEG), g)
 
         def tiles(i, g, tile):
-            acc = product(i, g)
-            for k in range(acc.shape[1] // TILE):
-                store_tile(parts, tile + k, acc[:, k * TILE:(k + 1) * TILE])
+            store_tile(parts, tile, product(i, g))
 
         def two(i):
             return pl.ds(pl.multiple_of(i * 2 * TILE, 2 * TILE), 2 * TILE)
@@ -875,11 +894,24 @@
             @pl.when(j == 0)
             def _():
                 weights_grad(0)
-                ex.step1_ab(0)
-
-            @pl.when((lax.rem(j, 2) == 0) & (j > 0))
+                ex.begin(0)
+
+            @pl.when(j == 2)
             def _():
-                ex.tick(j // 2 - 1)
+                ex.begin(1)
+
+            @pl.when(j == 3)
+            def _():
+                ex.tick(1)
+
+            @pl.when(j == 4)
+            def _():
+                ex.begin(2)
+
+            @pl.when(j == 5)
+            def _():
+                ex.tick(2)
+                ex.begin(3)
             return 0
 
         def weights_grad(j):
@@ -888,8 +920,12 @@
             tiles(0, m.act[rem(j, NG)], 8 * j)
             tiles(1, m.uc[rem(j, NG)], 8 * j + 4)
         lax.fori_loop(0, NFF, block, 0)
+        for n in range(2):
+            for cp in ring(n):
+                cp.start()
         weights_grad(NFF - 1)
         ex.tick(3)
+        ex.begin(4)
         for j in range(NFF - NG, NFF):
             for cp in ff_copies(j):
                 cp.wait_send()
@@ -909,65 +945,59 @@
         turn(2, 1, m.bc[...])
         at_copy(1, 0).wait_send()
         turn(5, 0, m.hn[...])
-        go_copy().wait_recv()
-        at_copy(2, 1).wait_recv()
-
-        def out_grad(i, _):
-            tiles(2, m.g_o[:, two(i)], 64 + 2 * i)
-            return 0
-        lax.fori_loop(0, 9, out_grad, 0)
+        def ring_next(n):
+            if n + 2 < 2 * E:
+                for cp in ring(n + 2):
+                    cp.start()
+
+        att = m.att[...].astype(F32)
+        seen = jnp.zeros((SEG, 128), F32)
+        total = jnp.zeros((SEG, HD), F32)
+        for e in range(E):
+            for cp in ring(e):
+                cp.wait()
+            cot = dot_nt(m.bc[...], m.wd[e % 2, :HD])
+            ring_next(e)
+            seen = seen + dot_nt((cot * att).astype(BF), m.exo[e, :128])
+            total = total + cot * gates_wide(m.exo, e)
+        m.ogc[...] = seen
+        m.ac[...] = total.astype(BF)
         ex.tick(4)
-
-        def through_output(wo):
-            load(11, wo_h, wo).wait()
-            m.acc[mem, :] = jnp.zeros((SEG, HD), F32)
-            m.ogc[...] = jnp.zeros((SEG, 128), F32)
-
-            def mixed(cols, _):
-                cot = dot_nt(m.bc[...], wo[cols, :])
-                seen = (cot * dot_nt(m.att[...], m.sel[cols, :HD])).astype(BF)
-                m.ogc[...] += dot_nt(seen, m.exo[:128, cols])
-                chosen = (cot * gates_wide(m.exo, cols)).astype(BF)
-                m.acc[mem, :] += dot(chosen, m.sel[cols, :HD])
-            for_wide(mixed)
-            m.att[...] = m.acc[mem, :].astype(BF)
-        pl.run_scoped(through_output, pltpu.VMEM((WIDE, D), BF))
-        ex.tick(5)
-
-        def values_back(h, _):
-            probs = weights_of(h)
-            cot = head_only(m.att[...], h)
-            m.acc[...] += dot_tn(probs.astype(BF), cot)
-            return 0
+        ex.begin(5)
 
         m.acc[...] = jnp.zeros((2 * SEG, HD), F32)
-        lax.fori_loop(0, H, values_back, 0)
-        m.vc[...] = m.acc[...].astype(BF)
-
-        @pl.when(t > 0)
-        def _():
-            vc_copy().start()
-        ex.tick(6)
-        m.acc[...] = jnp.zeros((2 * SEG, HD), F32)
+        m.acc2[...] = jnp.zeros((2 * SEG, HD), F32)
         m.qc[...] = jnp.zeros((SEG, HD), F32)
 
         def scores_back(h, _):
             probs = weights_of(h)
-            pc = dot_nt(head_only(m.att[...], h), m.v[...])
+            cot = head_only(m.ac[...], h)
+            m.acc2[...] += dot_tn(probs.astype(BF), cot)
+            pc = dot_nt(cot, m.v[...])
             sc = (probs * (pc - jnp.sum(probs * pc, axis=-1, keepdims=True))).astype(BF)
             m.qc[...] += dot(sc, head_only(m.k[...], h)) * scale
             m.acc[...] += dot_tn(sc, head_only(m.q[...], h)) * scale
             return 0
         lax.fori_loop(0, H, scores_back, 0)
+        m.vc[...] = m.acc2[...].astype(BF)
         m.kc[...] = m.acc[...].astype(BF)
 
         @pl.when(t > 0)
         def _():
+            vc_copy().start()
             kc_copy().start()
+        go_copy().wait_recv()
+        at_copy(2, 1).wait_recv()
+
+        def out_grad(i, _):
+            tiles(2, m.g_o[:, two(i)], 64 + 2 * i)
+            return 0
+        lax.fori_loop(0, 9, out_grad, 0)
         m.g_p[mem, HD:512] = jnp.zeros((SEG, 512 - HD), BF)
         m.g_p[mem, 512 + HD:1024] = jnp.zeros((SEG, 512 - HD), BF)
         m.g_p[mem, :HD] = m.qc[...].astype(BF)
-        ex.tick(7)
+        ex.tick(5)
+        ex.begin(6)
 
         @pl.when(t < last_t)
         def _():
@@ -983,46 +1013,48 @@
 
         own_cot, next_cot = m.mid, m.nsc
 
-        def through_values(wv, vg):
-            load(5, wv_h, wv).wait()
-            own_cot[...] = dot(m.kc[own, :], m.wk[...]) + dot(m.g_p[mem, :HD], m.wq[...])
-            next_cot[...] = dot(m.kn[...], m.wk[...])
-            vg[...] = jnp.zeros((2, SEG, 128), F32)
-
-            def values(cols, lo):
-                proj = dot_nt(m.xn[...], wv[cols, :])
-                gate = gates_wide(m.exv, cols)
-                vo = dot_nt(m.vc[own, :], m.sel[cols, :HD])
-                vn = dot_nt(m.vn[...], m.sel[cols, :HD])
-                for i, v in enumerate((vo, vn)):
-                    vg[i] += dot_nt((v * proj).astype(BF), m.exv[:128, cols])
-                po = (gate * vo).astype(BF)
-                pn = (gate * vn).astype(BF)
-                own_cot[...] += dot(po, wv[cols, :])
-                next_cot[...] += dot(pn, wv[cols, :])
-                both = (po.astype(F32) + pn.astype(F32)).astype(BF)
-                if isinstance(lo, int):
-                    m.g_p[mem, 1024 + lo:1024 + WIDE] = both
-                else:
-                    m.g_p[mem, pl.ds(pl.multiple_of(1024 + lo, WB), WB)] = both
-            for_wide(values)
-            slope = m.sig[...] * (1.0 - m.sig[...]) * m.hot[...]
-            lo_cot = ((vg[0] + m.ogc[...]) * slope).astype(BF)
-            ln_cot = (vg[1] * slope).astype(BF)
-            own_cot[...] += dot(lo_cot, m.wrp[...])
-            next_cot[...] += dot(ln_cot, m.wrp[...])
-            both = (lo_cot.astype(F32) + ln_cot.astype(F32)).astype(BF)
-            lane = lax.broadcasted_iota(jnp.int32, (SEG, 128), 1)
-            m.g_p[mem, 3200:3328] = jnp.where(lane < LOGIT, m.g_p[mem, 3200:3328], both)
-            gp_copy().start()
-
-            def norm1_back(rows):
-                unit, inv = unit_rows(m.x[rows, :].astype(F32))
-                cot = own_cot[rows, :]
-                m.lo[rows, :] += norm_back(unit, inv, cot * m.gains[0:1, :].astype(F32))
-                m.hn[rows, :] = ((cot + next_cot[rows, :]) * unit).astype(BF)
-            for_rows(32, norm1_back)
-        pl.run_scoped(through_values, pltpu.VMEM((WIDE, D), BF), pltpu.VMEM((2, SEG, 128), F32))
+        own_cot[...] = dot(m.kc[own, :], m.wk[...]) + dot(m.g_p[mem, :HD], m.wq[...])
+        next_cot[...] = dot(m.kn[...], m.wk[...])
+        m.vg[...] = jnp.zeros((2, SEG, 128), F32)
+        blocks = []
+        for e in range(E):
+            for cp in ring(E + e):
+                cp.wait()
+            wv = m.wd.at[(E + e) % 2]
+            proj = dot_nt(m.xn[...], wv[:HD])
+            gate = gates_wide(m.exv, e)
+            pair = []
+            for i, (v, acc) in enumerate(((m.vc[own, :], own_cot), (m.vn[...], next_cot))):
+                v = v.astype(F32)
+                m.vg[i] += dot_nt((v * proj).astype(BF), m.exv[e, :128])
+                pair.append((gate * v).astype(BF))
+                acc[...] += dot(pair[i], wv[:HD])
+            ring_next(E + e)
+            if e == 2:
+                ex.tick(6)
+                ex.begin(7)
+            blocks.append((pair[0].astype(F32) + pair[1].astype(F32)).astype(BF))
+            if e % 2 == 1 or e == E - 1:
+                first = e - 1 if e % 2 == 1 else e
+                m.g_p[mem, 1024 + first * HD:1024 + (e + 1) * HD] = side_by_side(blocks[first:])
+        slope = m.sig[...] * (1.0 - m.sig[...]) * m.hot[...]
+        lo_cot = ((m.vg[0] + m.ogc[...]) * slope).astype(BF)
+        ln_cot = (m.vg[1] * slope).astype(BF)
+        own_cot[...] += dot(lo_cot, m.wrp[...])
+        next_cot[...] += dot(ln_cot, m.wrp[...])
+        both = (lo_cot.astype(F32) + ln_cot.astype(F32)).astype(BF)
+        lane = lax.broadcasted_iota(jnp.int32, (SEG, 128), 1)
+        m.g_p[mem, 3200:3328] = jnp.where(lane < LOGIT, m.g_p[mem, 3200:3328], both)
+        gp_copy().start()
+        ex.tick(7)
+        ex.begin(8)
+
+        def norm1_back(rows):
+            unit, inv = unit_rows(m.x[rows, :].astype(F32))
+            cot = own_cot[rows, :]
+            m.lo[rows, :] += norm_back(unit, inv, cot * m.gains[0:1, :].astype(F32))
+            m.hn[rows, :] = ((cot + next_cot[rows, :]) * unit).astype(BF)
+        for_rows(32, norm1_back)
         l_ig = pltpu.make_async_copy(m.lo, ig_h, m.st.at[1])
         l_ig.start()
         at_copy(2, 1).wait_send()
@@ -1045,10 +1077,10 @@
             last += product(i, jnp.where(lane == at, 1.0, 0.0).astype(BF))
         store_tile(parts, 107, last)
 
-        def run(i, _):
+        ex.begin(9)
+        for i in range(9, NS + 5):
             ex.tick(i)
-            return 0
-        lax.fori_loop(9, NS + 5, run, 0)
+            ex.begin(i + 1)
         ex.finish()
         l_ig.wait()
 
@@ -1070,14 +1102,11 @@
 
 
 def tables():
-    col = np.arange(WIDE)
-    sel = (col // (E * DH) * DH + col % DH)[:, None] == np.arange(HD)[None, :]
-    branch = np.arange(128)[:, None]
-    exv = branch == LOGIT + col[None, :] // DH
-    exo = branch == LOGIT + H * E + col[None, :] // DH
-    exv, exo = (np.concatenate([v, v]) for v in (exv, exo))
-    sel = np.pad(sel, ((0, 0), (0, 512 - HD)))
-    exv, exo = (np.pad(v, ((0, 0), (0, 2304 - WIDE))) for v in (exv, exo))
+    col = np.arange(HD)[None, None, :] // DH * E + np.arange(E)[:, None, None]
+    branch = np.arange(128)[None, :, None]
+    exv = branch == LOGIT + col
+    exo = branch == LOGIT + H * E + col
+    exv, exo = (np.concatenate([v, v], axis=1) for v in (exv, exo))
     lane = np.arange(128) - LOGIT
     inside = (lane >= 0) & (lane < 2 * H * E)
     pick = (np.arange(2 * H)[:, None] == lane[None, :] // E) & inside
@@ -1085,13 +1114,13 @@
     spread[:2 * H, :128] = pick
     spread[16:16 + 2 * H, 128:] = pick
     spread[127, :128] = np.where(inside, lane % E, -1)
-    return tuple(v.astype(ml_dtypes.bfloat16) for v in (sel, exv, exo, spread))
+    return tuple(v.astype(ml_dtypes.bfloat16) for v in (exv, exo, spread))
 
 
 def fused_device(layer_input, routes, memory_lengths, norm_gains, w_query, w_key, w_value,
                  w_router, w_output, w_up, w_down, output_cot):
     anywhere = pl.BlockSpec(memory_space=pl.ANY)
-    specs = [anywhere] * 16
+    specs = [anywhere] * 15
     specs[2] = pl.BlockSpec(memory_space=pltpu.SMEM)
     out, grad, flat = pl.pallas_call(
         layer_kernel,
@@ -1129,11 +1158,15 @@
     for j in range(NFF):
         dd[:, j * FFB:(j + 1) * FFB] = flat[:, 2 * j * FFB:(2 * j + 1) * FFB]
         du[:, j * FFB:(j + 1) * FFB] = flat[:, (2 * j + 1) * FFB:(2 * j + 2) * FFB]
-    do[...] = flat[:, 2 * FF:2 * FF + WIDE]
     base = 82 * TILE
     dq[...] = flat[:, base:base + HD]
     dk[...] = flat[:, base + 512:base + 512 + HD]
-    dv[...] = flat[:, base + 1024:base + 1024 + WIDE]
+    for h in range(H):
+        for e in range(E):
+            to = slice((h * E + e) * DH, (h * E + e + 1) * DH)
+            at = e * HD + h * DH
+            do[:, to] = flat[:, 2 * FF + at:2 * FF + at + DH]
+            dv[:, to] = flat[:, base + 1024 + at:base + 1024 + at + DH]
     tail = flat[:, 107 * TILE:108 * TILE]
     dr[...] = tail[:, LOGIT:LOGIT + 2 * H * E]
     gains[...] = jnp.transpose(tail)[104:106, :]

time: 167 us -> 150 us (0.90)
  Pallas kernels: 165 us -> 148 us
    pallas_call x1, Pallas kernels: 162 us -> 145 us  [fused_device(): pl.pallas_call(layer_kernel, out_shape=(jax.ShapeDtypeStruct((SEG, D), BF...]
where the time goes in v2:
time: 150 us
  Pallas kernels  148 us (99%)
    pallas_call x1, Pallas kernels, fused_device(): pl.pallas_call(layer_kernel, out_shape=(jax.ShapeDtypeStruct((SEG, D), BF...  145 us
    pallas_call x1, Pallas kernels, fused_device(): pl.pallas_call(split_kernel, out_shape=tuple((jax.ShapeDtypeStruct(*v) fo...  3.68 us

profile of v2, /device:TPU:0, one launch (start us, length us, event | category | flops | bytes accessed | tf_op | source)
XLA Modules:
  0.0 149.9 jit_solution(17307774875061250713)
XLA Ops:
  1.3 144.7 %layer.1 = (bf16[256,1024]{1,0:T(8,128)(2,1)}, f32[256,1024]{1,0:T(8,128)}, f32[32,13824]{1,0:T(8,128)}) custom-call(bf16[256,1024]{1,0:T(8,128)(2,1)} %bitcast.16, s32[8,2,256]{2,1,0:T(2,128)} %bitcast.19, s32[1,1]{1,0:T(1,128)S(6)} %copy.25.len_s, bf16[2,1024]{1,0:T(2,128)(2,1)} %gains_h.1, bf16[448,1024]{1,0:T(8,128)(2,1)} %bitcast.14, ...), custom_call_target="tpu_custom_call" | custom-call | tf_op jit(solution)/shard_map/layer/pallas_call | solution.py:1125
  146.0 3.7 %split.1 = (bf16[256,1024]{1,0:T(8,128)(2,1)}, f32[256,1024]{1,0:T(8,128)}, f32[2,32]{1,0:T(2,128)}, f32[32,448]{1,0:T(8,128)}, f32[32,448]{1,0:T(8,128)}, /*ind...) custom-call(bf16[256,1024]{1,0:T(8,128)(2,1)} %get-tuple-element.23.out_h, ...), custom_call_target="tpu_custom_call" | custom-call | tf_op jit(solution)/shard_map/split/pallas_call | solution.py:1140

commit v3 on v2

--- a/solution.py
+++ b/solution.py
@@ -254,7 +254,7 @@
 
 MESH_ID = pl.DeviceIdType.MESH
 TILE = 128
-PIECES = [(6, 2)] * 2 + [(7, 2)] * 8 + [(5, 2), (4, 1), (3, 1), (2, 0), (2, 0)]
+PIECES = [(4, 2), (7, 2), (6, 2), (7, 2), (7, 2), (6, 2), (7, 2), (7, 2), (7, 2), (6, 2), (5, 2), (5, 2), (5, 1), (3, 1)]
 NS = len(PIECES)
 TILES = sum(a + b for a, b in PIECES)
 FLAT = TILES * TILE
@@ -263,14 +263,48 @@
 MOST = max(a + b for a, b in PIECES) * TILE
 N1 = 6
 NR = 4
-NZ = 7
+NZ = 6
+NZ1 = 7
 HALF = (slice(0, 16), slice(16, 32))
+
+
+POINTS = ([("d0", 4), ("u0", 8), ("j1", 16)] + [(f"j{j}", 8 * j) for j in range(2, 8)] + [("dw7", 64), ("ln2b", 64)]
+          + [(f"tho{e}", 64) for e in range(E)] + [("sb0", 64), ("sb1", 64), ("dwo0", 70), ("dwo1", 76), ("dwo2", 82)]
+          + [(f"tv{e}", 82) for e in range(E)] + [("ln1b", 82), ("dwp0", 90), ("dwp1", 98), ("dwp2", 108)])
+ROUNDS = ['j2', 'j4', 'j6', 'tho0', 'sb0', 'dwo1', 'tv1', 'tv4', 'dwp1']
+
+
+def plan():
+    ends = [sum(a + b for a, b in PIECES[:p + 1]) for p in range(NS)]
+    begun, t, todo = 0, 1, {}
+    for name, ready in POINTS:
+        ops = todo[name] = []
+        for again in range(1 + ROUNDS.count(name)):
+            if again:
+                assert begun >= t
+                ops.append(("round", t))
+                t += 1
+            while begun < NS and ends[begun] <= ready and (begun <= t or begun < 3):
+                ops.append(("begin", begun))
+                begun += 1
+    rest = []
+    while t < NS + 5:
+        rest.append(("round", t))
+        t += 1
+        while begun < NS and begun <= t:
+            rest.append(("begin", begun))
+            begun += 1
+    todo["rest"] = rest
+    return todo
+
+
+PLAN = plan()
 
 
 class Piece:
     def __init__(self, p):
         start = sum(a + b for a, b in PIECES[:p]) * TILE
-        self.p, self.f, self.r, self.q = p, p % N1, p % NR, p % NZ
+        self.p, self.f, self.r, self.q, self.g = p, p % N1, p % NR, p % NZ, p % NZ1
         self.wf, self.wl = (v * TILE for v in PIECES[p])
         self.first = slice(start, start + self.wf)
         self.last = slice(start + self.wf, start + self.wf + self.wl)
@@ -337,10 +371,10 @@
         return self.copy(7, g, self.parts.at[self.s, 0:z, self.y, :, g.first], self.zd.at[g.q, 0:z, :, :g.wf], self.to_down)
 
     def c_upc(self, g, z):
-        return self.copy(8, g, self.parts.at[:, z + 1:4, :, :, g.last], self.zuc.at[g.q, :, z:3, :, :, :g.wl], self.to_up)
+        return self.copy(8, g, self.parts.at[:, z + 1:4, :, :, g.last], self.zuc.at[g.g, :, z:3, :, :, :g.wl], self.to_up)
 
     def c_downc(self, g, z):
-        return self.copy(9, g, self.parts.at[:, 0:z, :, :, g.last], self.zdc.at[g.q, :, 0:z, :, :, :g.wl], self.to_down)
+        return self.copy(9, g, self.parts.at[:, 0:z, :, :, g.last], self.zdc.at[g.g, :, 0:z, :, :, :g.wl], self.to_down)
 
     def add(self, at, cols, value):
         self.parts[(*at, cols)] = self.parts[(*at, cols)] + value
@@ -355,7 +389,7 @@
             if is_c:
                 def body(i, _):
                     a, b = i // 2, i % 2
-                    self.add((a, u, b, rows), g.last, src[g.q, a, at, b, :, :g.wl])
+                    self.add((a, u, b, rows), g.last, src[g.g, a, at, b, :, :g.wl])
                     return 0
                 lax.fori_loop(0, 4, body, 0)
             else:
@@ -429,7 +463,7 @@
         def _():
             def body(i, _):
                 a, b = i // 2, i % 2
-                self.add((a, z, b, rows), g.last, self.zuc[g.q, a, z - 1, b, :, :g.wl])
+                self.add((a, z, b, rows), g.last, self.zuc[g.g, a, z - 1, b, :, :g.wl])
                 return 0
             lax.fori_loop(0, 4, body, 0)
 
@@ -437,7 +471,7 @@
         def _():
             def body(i, _):
                 a, b = i // 2, i % 2
-                self.add((a, z, b, rows), g.last, self.zdc[g.q, a, z, b, :, :g.wl])
+                self.add((a, z, b, rows), g.last, self.zdc[g.g, a, z, b, :, :g.wl])
                 return 0
             lax.fori_loop(0, 4, body, 0)
         self.c_xc(g).start()
@@ -487,9 +521,9 @@
             if 0 <= t - 1 - k < NS:
                 step(Piece(t - 1 - k))
 
-    def begin(self, p):
-        if p < NS:
-            self.step1(Piece(p))
+    def serve(self, point):
+        for what, n in PLAN[point]:
+            self.tick(n) if what == "round" else self.step1(Piece(n))
 
     def finish(self):
         self.c_out(Piece(NS - 2)).wait()
@@ -526,8 +560,8 @@
     pltpu.VMEM((NR, 4, 16, MOST_FIRST), jnp.bfloat16),
     pltpu.VMEM((NZ, 3, 32, MOST_FIRST), jnp.bfloat16),
     pltpu.VMEM((NZ, 3, 32, MOST_FIRST), jnp.bfloat16),
-    pltpu.VMEM((NZ, 2, 3, 2, 32, MOST_LAST), jnp.bfloat16),
-    pltpu.VMEM((NZ, 2, 3, 2, 32, MOST_LAST), jnp.bfloat16),
+    pltpu.VMEM((NZ1, 2, 3, 2, 32, MOST_LAST), jnp.bfloat16),
+    pltpu.VMEM((NZ1, 2, 3, 2, 32, MOST_LAST), jnp.bfloat16),
     pltpu.VMEM((NR, 2, 32, MOST_LAST), jnp.bfloat16),
     pltpu.VMEM((NR, 32, MOST_LAST), jnp.bfloat16),
 ]
@@ -562,6 +596,7 @@
 FF = 4096
 SEG = 256
 HD = H * DH
+HH = HD // 2
 WIDE = H * E * DH
 FFB = 512
 NFF = FF // FFB
@@ -601,6 +636,13 @@
                   - unit * jnp.mean(cot * unit, axis=-1, keepdims=True))
 
 
+def normal_cdf(v, bell):
+    u = 1.0 / (1.0 + 0.23164189 * jnp.abs(v))
+    poly = ((((0.5307027145 * u - 0.7265760135) * u + 0.7107068705) * u - 0.142248368) * u + 0.127414796) * u
+    tail = poly * bell
+    return jnp.where(v < 0.0, tail, 1.0 - tail)
+
+
 def for_rows(step, body):
     def inner(i, _):
         body(pl.ds(pl.multiple_of(i * step, step), step))
@@ -615,7 +657,7 @@
 NAMES = (
     "x", "oc", "gains", "rt", "rf", "spread", "hot", "wq", "wk", "wr", "wrp", "wu", "wd", "exv", "exo",
     "xn", "hn", "mid", "lo", "nsc", "q", "k", "v", "sig", "att", "acc", "g_o", "g_p",
-    "act", "uc", "bc", "kc", "vc", "kn", "vn", "ob", "gg", "ogc", "qc", "vg", "ac", "acc2",
+    "act", "uc", "bc", "kc", "vc", "kn", "vn", "ob", "gg", "ogc", "qc", "vg", "ac", "acc2", "up",
     "at", "full",
     "ld", "ld2", "lde", "kv_s", "kv_r", "sib_s", "sib_r", "st", "stage", "out_sem", "ssem", "rsem",
 )
@@ -628,21 +670,22 @@
         v((SEG, D), BF), v((SEG, D), BF), v((2, D), BF), v((2 * H, 2, SEG), jnp.int32), v((128, SEG), BF),
         v((128, 256), BF), v((SEG, 128), F32),
         v((HD, D), BF), v((HD, D), BF), v((2 * H * E, D), BF), v((128, D), BF),
-        v((2, D, FFB), BF), v((2, FFB, D), BF), v((E, 256, HD), BF), v((E, 256, HD), BF),
+        v((2, D, FFB), BF), v((2, FFB, D), BF), v((2, E, 256, HH), BF), v((2, E, 256, HH), BF),
         v((SEG, D), BF), v((SEG, D), BF), v((SEG, D), F32), v((SEG, D), F32), v((SEG, D), F32),
-        v((SEG, HD), BF), v((2 * SEG, HD), BF), v((2 * SEG, HD), BF), v((SEG, 128), F32),
-        v((SEG, HD), BF), v((2 * SEG, HD), F32), v((2 * SEG, 2304), BF), v((2 * SEG, 3328), BF),
+        v((2, SEG, HH), BF), v((2, 2 * SEG, HH), BF), v((2, 2 * SEG, HH), BF), v((SEG, 128), F32),
+        v((2, SEG, HH), BF), v((2, 2 * SEG, HH), F32), v((2 * SEG, 2304), BF), v((2 * SEG, 3328), BF),
         v((NG, 2 * SEG, FFB), BF), v((NG, 2 * SEG, FFB), BF), v((SEG, D), BF),
-        v((2 * SEG, HD), BF), v((2 * SEG, HD), BF), v((SEG, HD), BF), v((SEG, HD), BF), v((SEG, D), BF), v((SEG, 256), BF), v((SEG, 128), F32), v((SEG, HD), F32), v((2, SEG, 128), F32),
-        v((SEG, HD), BF), v((2 * SEG, HD), F32),
+        v((2, 2 * SEG, HH), BF), v((2, 2 * SEG, HH), BF), v((2, SEG, HH), BF), v((2, SEG, HH), BF), v((SEG, D), BF), v((SEG, 256), BF),
+        v((SEG, 128), F32), v((2, SEG, HH), F32), v((2, SEG, 128), F32),
+        v((2, SEG, HH), BF), v((2, 2 * SEG, HH), F32), v((SEG, FFB), F32),
         v((6, 16, 32, 2 * SEG), BF), v((2, 16, 2, 32, SEG), BF),
-        dma((16,)), dma((4,)), dma((2, 2 * E)), dma((4,)), dma((4,)), dma((OWN_SIB,)), dma((OWN_SIB,)), dma((2,)),
+        dma((16,)), dma((4,)), dma((2, 2 * E)), dma((5,)), dma((5,)), dma((OWN_SIB,)), dma((OWN_SIB,)), dma((2,)),
         v((2, 32, MOST), F32), dma((2,)), dma((10, NS)), dma((10, NS)),
     ]
 
 
 def layer_kernel(x_h, rt_h, len_s, gains_h, wq_h, wk_h, wv_h, wr_h, wo_h, wu_h, wd_h, oc_h,
-                 exv_h, exo_h, spread_h, lo_h, ig_h, flat_h, *scratch):
+                 spread_h, lo_h, ig_h, flat_h, *scratch):
     m = types.SimpleNamespace(**dict(zip(NAMES, scratch[:len(NAMES)])))
     recv = scratch[len(NAMES):]
     s, t, z, y, c = place()
@@ -679,14 +722,26 @@
         return sibling(7, m.g_p.at[mem], m.g_p.at[own])
 
     def ff_copies(j):
+        return act_copy(j), uc_copy(j)
+
+    def act_copy(j):
         g = rem(j, NG)
-        return (sibling(8 + 2 * j, m.act.at[g, mem], m.act.at[g, own]),
-                sibling(9 + 2 * j, m.uc.at[g, mem], m.uc.at[g, own]))
+        return sibling(8 + 2 * j, m.act.at[g, mem], m.act.at[g, own])
+
+    def uc_copy(j):
+        g = rem(j, NG)
+        return sibling(9 + 2 * j, m.uc.at[g, mem], m.uc.at[g, own])
 
     def ff_loads(j):
+        return wu_load(j), wd_load(j)
+
+    def wu_load(j):
         cols = pl.ds(pl.multiple_of(j * FFB, FFB), FFB)
-        return (pltpu.make_async_copy(wu_h.at[:, cols], m.wu.at[j % 2], m.ld2.at[j % 2]),
-                pltpu.make_async_copy(wd_h.at[cols, :], m.wd.at[j % 2], m.ld2.at[2 + j % 2]))
+        return pltpu.make_async_copy(wu_h.at[:, cols], m.wu.at[rem(j, 2)], m.ld2.at[rem(j, 2)])
+
+    def wd_load(j):
+        rows = pl.ds(pl.multiple_of(j * FFB, FFB), FFB)
+        return pltpu.make_async_copy(wd_h.at[rows, :], m.wd.at[rem(j, 2)], m.ld2.at[2 + rem(j, 2)])
 
     def along(i, src, dst, by):
         return pltpu.make_async_remote_copy(
@@ -694,26 +749,35 @@
             device_id={"seq": s, "tm": t + by}, device_id_type=MESH_ID)
 
     def k_copy():
-        return along(0, m.k.at[own], m.k.at[mem], 1)
-
-    def v_copy():
-        return along(1, m.v.at[own], m.v.at[mem], 1)
+        return along(0, m.k.at[:, own], m.k.at[:, mem], 1)
+
+    def v_copy(half):
+        return along(1 + half, m.v.at[half, own], m.v.at[half, mem], 1)
 
     def kc_copy():
-        return along(2, m.kc.at[mem], m.kn, -1)
+        return along(3, m.kc.at[:, mem], m.kn, -1)
 
     def vc_copy():
-        return along(3, m.vc.at[mem], m.vn, -1)
-
-    def head_lanes(rows, h):
-        lane = lax.broadcasted_iota(jnp.int32, (rows, HD), 1)
-        return (lane >= h * DH) & (lane < (h + 1) * DH)
+        return along(4, m.vc.at[:, mem], m.vn, -1)
+
+    def half_rows(half):
+        return slice(half * HH, (half + 1) * HH)
 
     def head_only(v, h):
-        return jnp.where(head_lanes(v.shape[0], h), v, jnp.zeros_like(v))
-
-    def gates_wide(table, e):
-        return dot(m.gg[...], table[e])
+        lane = lax.broadcasted_iota(jnp.int32, v.shape, 1)
+        lo = rem(h, 2) * DH
+        return jnp.where((lane >= lo) & (lane < lo + DH), v, jnp.zeros_like(v))
+
+    def gates_wide(table, half, e):
+        return dot(m.gg[...], table[half, e])
+
+    def make_table(table, first):
+        row = lax.broadcasted_iota(jnp.int32, (256, HH), 0)
+        lane = lax.broadcasted_iota(jnp.int32, (256, HH), 1)
+        row = jnp.where(row >= 128, row - 128, row) - first - jnp.where(lane >= DH, E, 0)
+        for half in range(2):
+            for e in range(E):
+                table[half, e] = jnp.where(row == 2 * E * half + e, 1.0, 0.0).astype(BF)
 
     def expert_loads(which, n, e, src, dst):
         return [pltpu.make_async_copy(src.at[pl.ds((h * E + e) * DH, DH)], dst.at[pl.ds(h * DH, DH)], m.lde.at[which, n])
@@ -723,7 +787,8 @@
         return expert_loads(0, n, n % E, wo_h if n < E else wv_h, m.wd.at[n % 2])
 
     def weights_of(h):
-        scores = dot_nt(head_only(m.q[...], h), m.k[...]) * scale
+        half = h // 2
+        scores = dot_nt(head_only(m.q[half], h), m.k[half]) * scale
         length = len_s[0, 0]
         row = lax.broadcasted_iota(jnp.int32, (SEG, 2 * SEG), 0)
         col = lax.broadcasted_iota(jnp.int32, (SEG, 2 * SEG), 1)
@@ -739,12 +804,12 @@
     l_rt = load(4, rt_h, m.rt)
     l_sp = load(12, spread_h, m.spread)
 
-    def forward(wv, wo):
-        l_ev = load(6, exv_h, m.exv)
+    def forward(wv, wo, wide):
         l_v = [expert_loads(0, e, e, wv_h, wv.at[e]) for e in range(E)]
         for group in l_v:
             for cp in group:
                 cp.start()
+        make_table(m.exv, LOGIT)
         l_x.wait()
         l_g.wait()
 
@@ -753,11 +818,11 @@
             m.xn[rows, :] = (unit * m.gains[0:1, :].astype(F32)).astype(BF)
         for_rows(32, norm1)
         l_k.wait()
-        m.k[own, :] = dot_nt(m.xn[...], m.wk[...]).astype(BF)
+        for half in range(2):
+            m.k[half, own] = dot_nt(m.xn[...], m.wk[half_rows(half), :]).astype(BF)
         l_q = load(8, wq_h, m.wq)
         l_oc = load(9, oc_h, m.oc)
-        l_eo = load(10, exo_h, m.exo)
-        l_wo = [expert_loads(1, e, e, wo_h, wo.at[e]) for e in range(E)]
+        l_wo = [expert_loads(1, e, e, wo_h, wo.at[pl.ds(e * HD, HD)]) for e in range(E)]
         for group in l_wo:
             for cp in group:
                 cp.start()
@@ -786,22 +851,25 @@
         top, low = halves(sig * m.hot[...])
         m.gg[:, :128] = top
         m.gg[:, 128:] = low
-        l_ev.wait()
-        total = jnp.zeros((SEG, HD), F32)
-        for e in range(E):
-            for cp in l_v[e]:
-                cp.wait()
-            total = total + dot_nt(m.xn[...], wv[e]) * gates_wide(m.exv, e)
-        m.v[own, :] = total.astype(BF)
-
-        @pl.when(t < last_t)
-        def _():
-            v_copy().start()
+        for half in range(2):
+            total = jnp.zeros((SEG, HH), F32)
+            for e in range(E):
+                if half == 0:
+                    for cp in l_v[e]:
+                        cp.wait()
+                total = total + dot_nt(m.xn[...], wv[e, half_rows(half)]) * gates_wide(m.exv, half, e)
+            m.v[half, own] = total.astype(BF)
+
+            @pl.when(t < last_t)
+            def _():
+                v_copy(half).start()
         l_q.wait()
-        m.q[...] = dot_nt(m.xn[...], m.wq[...]).astype(BF)
+        for half in range(2):
+            m.q[half] = dot_nt(m.xn[...], m.wq[half_rows(half), :]).astype(BF)
         l_oc.wait()
         turn(0, 0, m.oc[...])
         turn(3, 1, m.xn[...])
+        make_table(m.exo, LOGIT + H * E)
 
         @pl.when(t > 0)
         def _():
@@ -809,31 +877,34 @@
 
         @pl.when(t == 0)
         def _():
-            m.k[mem, :] = jnp.zeros((SEG, HD), BF)
-            m.v[mem, :] = jnp.zeros((SEG, HD), BF)
+            m.k[:, mem] = jnp.zeros((2, SEG, HH), BF)
+            m.v[:, mem] = jnp.zeros((2, SEG, HH), BF)
         for h in range(H):
             m.act[h, mem] = weights_of(h).astype(BF)
-
-        @pl.when(t > 0)
-        def _():
-            v_copy().wait_recv()
-        total = jnp.zeros((SEG, HD), F32)
-        for h in range(H):
-            total = total + dot(m.act[h, mem], head_only(m.v[...], h))
-        m.att[...] = total.astype(BF)
-        l_eo.wait()
+        for half in range(2):
+            for e in range(E):
+                wide[half, e] = gates_wide(m.exo, half, e)
+        for cp in ff_loads(0):
+            cp.wait()
+        m.up[...] = dot_nt(m.oc[...], m.wd[0])
         m.g_o[mem, 2176:2304] = jnp.zeros((SEG, 128), BF)
-        total = m.x[...].astype(F32)
-        blocks = []
-        for e in range(E):
-            blocks.append((gates_wide(m.exo, e) * m.att[...].astype(F32)).astype(BF))
-            for cp in l_wo[e]:
+        for half in range(2):
+            @pl.when(t > 0)
+            def _():
+                v_copy(half).wait_recv()
+            total = jnp.zeros((SEG, HH), F32)
+            for h in (2 * half, 2 * half + 1):
+                total = total + dot(m.act[h, mem], head_only(m.v[half], h))
+            m.att[half] = total.astype(BF)
+        att = [m.att[half].astype(F32) for half in range(2)]
+        for e in range(0, E, 2):
+            blocks = [(wide[half, i] * att[half]).astype(BF) for i in range(e, min(e + 2, E)) for half in range(2)]
+            m.g_o[mem, e * HD:min(e + 2, E) * HD] = side_by_side(blocks)
+        go_copy().start()
+        for group in l_wo:
+            for cp in group:
                 cp.wait()
-            total = total + dot(blocks[e], wo[e])
-        m.mid[...] = total
-        for e in range(0, E, 2):
-            m.g_o[mem, e * HD:min(e + 2, E) * HD] = side_by_side(blocks[e:e + 2])
-        go_copy().start()
+        m.mid[...] = m.x[...].astype(F32) + dot(m.g_o[mem, :WIDE], wo[...])
 
         def norm2(rows):
             unit, _ = unit_rows(m.mid[rows, :])
@@ -842,7 +913,7 @@
         at_copy(0, 0).wait_send()
         turn(1, 0, m.hn[...])
 
-    pl.run_scoped(forward, pltpu.VMEM((E, HD, D), BF), pltpu.VMEM((E, HD, D), BF))
+    pl.run_scoped(forward, pltpu.VMEM((E, HD, D), BF), pltpu.VMEM((WIDE, D), BF), pltpu.VMEM((2, E, SEG, HH), F32))
 
     def backward(parts):
         ex = Exchange(parts, recv, (m.ssem, m.rsem), m.stage, m.out_sem, flat_h)
@@ -852,9 +923,6 @@
 
         def tiles(i, g, tile):
             store_tile(parts, tile, product(i, g))
-
-        def two(i):
-            return pl.ds(pl.multiple_of(i * 2 * TILE, 2 * TILE), 2 * TILE)
 
         m.lo[...] = m.mid[...]
         m.nsc[...] = jnp.zeros((SEG, D), F32)
@@ -864,25 +932,28 @@
         def block(j, _):
             b = rem(j, 2)
             g = rem(j, NG)
-            for cp in ff_loads(j):
-                cp.wait()
-            pre = dot(m.hn[...], m.wu[b])
-            cdf = 0.5 * (1.0 + lax.erf(pre * 0.7071067811865476))
-            pdf = jnp.exp(-0.5 * pre * pre) * 0.3989422804014327
-            up = dot_nt(m.oc[...], m.wd[b])
+
+            @pl.when(j > 0)
+            def _():
+                wu_load(j).wait()
 
             @pl.when(j >= NG)
             def _():
                 for cp in ff_copies(j - NG):
                     cp.wait_send()
+            pre = dot(m.hn[...], m.wu[b])
+            bell = jnp.exp(-0.5 * pre * pre)
+            cdf = normal_cdf(pre, bell)
             m.act[g, mem] = (pre * cdf).astype(BF)
-            m.uc[g, mem] = (up * (cdf + pre * pdf)).astype(BF)
-            for cp in ff_copies(j):
-                cp.start()
-
-            @pl.when(j > 1)
+            act_copy(j).start()
+            pdf = bell * 0.3989422804014327
+            m.uc[g, mem] = (m.up[...] * (cdf + pre * pdf)).astype(BF)
+            uc_copy(j).start()
+
+            @pl.when(j > 2)
             def _():
-                weights_grad(j - 1)
+                act_grad(j - 1)
+                up_grad(j - 1)
             m.lo[...] += dot(m.act[g, mem], m.wd[b])
             m.nsc[...] += dot_nt(m.uc[g, mem], m.wu[b])
 
@@ -893,39 +964,39 @@
 
             @pl.when(j == 0)
             def _():
-                weights_grad(0)
-                ex.begin(0)
-
-            @pl.when(j == 2)
+                act_grad(0)
+                ex.serve("d0")
+                up_grad(0)
+                ex.serve("u0")
+
+            @pl.when(j + 1 < NFF)
             def _():
-                ex.begin(1)
-
-            @pl.when(j == 3)
+                wd_load(j + 1).wait()
+                m.up[...] = dot_nt(m.oc[...], m.wd[rem(j + 1, 2)])
+
+            @pl.when(j == 1)
             def _():
-                ex.tick(1)
-
-            @pl.when(j == 4)
-            def _():
-                ex.begin(2)
-
-            @pl.when(j == 5)
-            def _():
-                ex.tick(2)
-                ex.begin(3)
+                act_grad(1)
+                up_grad(1)
+            for i in range(1, NFF):
+                if PLAN[f"j{i}"]:
+                    pl.when(j == i)(lambda i=i: ex.serve(f"j{i}"))
             return 0
 
-        def weights_grad(j):
-            for cp in ff_copies(j):
-                cp.wait_recv()
+        def act_grad(j):
+            act_copy(j).wait_recv()
             tiles(0, m.act[rem(j, NG)], 8 * j)
+
+        def up_grad(j):
+            uc_copy(j).wait_recv()
             tiles(1, m.uc[rem(j, NG)], 8 * j + 4)
         lax.fori_loop(0, NFF, block, 0)
         for n in range(2):
             for cp in ring(n):
                 cp.start()
-        weights_grad(NFF - 1)
-        ex.tick(3)
-        ex.begin(4)
+        act_grad(NFF - 1)
+        up_grad(NFF - 1)
+        ex.serve("dw7")
         for j in range(NFF - NG, NFF):
             for cp in ff_copies(j):
                 cp.wait_send()
@@ -945,40 +1016,46 @@
         turn(2, 1, m.bc[...])
         at_copy(1, 0).wait_send()
         turn(5, 0, m.hn[...])
+        ex.serve("ln2b")
+
         def ring_next(n):
             if n + 2 < 2 * E:
                 for cp in ring(n + 2):
                     cp.start()
 
-        att = m.att[...].astype(F32)
+        att = [m.att[half].astype(F32) for half in range(2)]
         seen = jnp.zeros((SEG, 128), F32)
-        total = jnp.zeros((SEG, HD), F32)
+        total = [jnp.zeros((SEG, HH), F32)] * 2
         for e in range(E):
             for cp in ring(e):
                 cp.wait()
-            cot = dot_nt(m.bc[...], m.wd[e % 2, :HD])
+            cots = [dot_nt(m.bc[...], m.wd[e % 2, half_rows(half)]) for half in range(2)]
             ring_next(e)
-            seen = seen + dot_nt((cot * att).astype(BF), m.exo[e, :128])
-            total = total + cot * gates_wide(m.exo, e)
+            for half, cot in enumerate(cots):
+                seen = seen + dot_nt((cot * att[half]).astype(BF), m.exo[half, e, :128])
+                total[half] = total[half] + cot * gates_wide(m.exo, half, e)
+            ex.serve(f"tho{e}")
         m.ogc[...] = seen
-        m.ac[...] = total.astype(BF)
-        ex.tick(4)
-        ex.begin(5)
-
-        m.acc[...] = jnp.zeros((2 * SEG, HD), F32)
-        m.acc2[...] = jnp.zeros((2 * SEG, HD), F32)
-        m.qc[...] = jnp.zeros((SEG, HD), F32)
-
-        def scores_back(h, _):
+        for half in range(2):
+            m.ac[half] = total[half].astype(BF)
+
+        m.acc[...] = jnp.zeros((2, 2 * SEG, HH), F32)
+        m.acc2[...] = jnp.zeros((2, 2 * SEG, HH), F32)
+        m.qc[...] = jnp.zeros((2, SEG, HH), F32)
+
+        def scores_back(h):
+            half = h // 2
             probs = weights_of(h)
-            cot = head_only(m.ac[...], h)
-            m.acc2[...] += dot_tn(probs.astype(BF), cot)
-            pc = dot_nt(cot, m.v[...])
+            cot = head_only(m.ac[half], h)
+            m.acc2[half] += dot_tn(probs.astype(BF), cot)
+            pc = dot_nt(cot, m.v[half])
             sc = (probs * (pc - jnp.sum(probs * pc, axis=-1, keepdims=True))).astype(BF)
-            m.qc[...] += dot(sc, head_only(m.k[...], h)) * scale
-            m.acc[...] += dot_tn(sc, head_only(m.q[...], h)) * scale
-            return 0
-        lax.fori_loop(0, H, scores_back, 0)
+            m.qc[half] += dot(sc, head_only(m.k[half], h)) * scale
+            m.acc[half] += dot_tn(sc, head_only(m.q[half], h)) * scale
+        for i in range(2):
+            scores_back(2 * i)
+            scores_back(2 * i + 1)
+            ex.serve(f"sb{i}")
         m.vc[...] = m.acc2[...].astype(BF)
         m.kc[...] = m.acc[...].astype(BF)
 
@@ -989,15 +1066,12 @@
         go_copy().wait_recv()
         at_copy(2, 1).wait_recv()
 
-        def out_grad(i, _):
-            tiles(2, m.g_o[:, two(i)], 64 + 2 * i)
-            return 0
-        lax.fori_loop(0, 9, out_grad, 0)
+        for i in range(3):
+            tiles(2, m.g_o[:, 6 * TILE * i:6 * TILE * (i + 1)], 64 + 6 * i)
+            ex.serve(f"dwo{i}")
         m.g_p[mem, HD:512] = jnp.zeros((SEG, 512 - HD), BF)
         m.g_p[mem, 512 + HD:1024] = jnp.zeros((SEG, 512 - HD), BF)
-        m.g_p[mem, :HD] = m.qc[...].astype(BF)
-        ex.tick(5)
-        ex.begin(6)
+        m.g_p[mem, :HD] = side_by_side([m.qc[half].astype(BF) for half in range(2)])
 
         @pl.when(t < last_t)
         def _():
@@ -1006,37 +1080,41 @@
 
         @pl.when(t == last_t)
         def _():
-            m.kn[...] = jnp.zeros((SEG, HD), BF)
-            m.vn[...] = jnp.zeros((SEG, HD), BF)
-        m.g_p[mem, 512:512 + HD] = (m.kc[own, :].astype(F32) + m.kn[...].astype(F32)).astype(BF)
+            m.kn[...] = jnp.zeros((2, SEG, HH), BF)
+            m.vn[...] = jnp.zeros((2, SEG, HH), BF)
+        m.g_p[mem, 512:512 + HD] = side_by_side(
+            [(m.kc[half, own].astype(F32) + m.kn[half].astype(F32)).astype(BF) for half in range(2)])
         l_lo.wait()
 
         own_cot, next_cot = m.mid, m.nsc
 
-        own_cot[...] = dot(m.kc[own, :], m.wk[...]) + dot(m.g_p[mem, :HD], m.wq[...])
-        next_cot[...] = dot(m.kn[...], m.wk[...])
+        own_cot[...] = (dot(m.g_p[mem, :HD], m.wq[...])
+                        + sum(dot(m.kc[half, own], m.wk[half_rows(half), :]) for half in range(2)))
+        next_cot[...] = sum(dot(m.kn[half], m.wk[half_rows(half), :]) for half in range(2))
         m.vg[...] = jnp.zeros((2, SEG, 128), F32)
         blocks = []
         for e in range(E):
             for cp in ring(E + e):
                 cp.wait()
             wv = m.wd.at[(E + e) % 2]
-            proj = dot_nt(m.xn[...], wv[:HD])
-            gate = gates_wide(m.exv, e)
-            pair = []
-            for i, (v, acc) in enumerate(((m.vc[own, :], own_cot), (m.vn[...], next_cot))):
-                v = v.astype(F32)
-                m.vg[i] += dot_nt((v * proj).astype(BF), m.exv[e, :128])
-                pair.append((gate * v).astype(BF))
-                acc[...] += dot(pair[i], wv[:HD])
+            pairs = []
+            for half in range(2):
+                proj = dot_nt(m.xn[...], wv[half_rows(half)])
+                gate = gates_wide(m.exv, half, e)
+                pair = []
+                for i, v in enumerate((m.vc[half, own], m.vn[half])):
+                    v = v.astype(F32)
+                    m.vg[i] += dot_nt((v * proj).astype(BF), m.exv[half, e, :128])
+                    pair.append((gate * v).astype(BF))
+                blocks.append((pair[0].astype(F32) + pair[1].astype(F32)).astype(BF))
+                pairs.append(pair)
+            for i, acc in enumerate((own_cot, next_cot)):
+                acc[...] += dot(side_by_side([pair[i] for pair in pairs]), wv[:HD])
             ring_next(E + e)
-            if e == 2:
-                ex.tick(6)
-                ex.begin(7)
-            blocks.append((pair[0].astype(F32) + pair[1].astype(F32)).astype(BF))
+            ex.serve(f"tv{e}")
             if e % 2 == 1 or e == E - 1:
                 first = e - 1 if e % 2 == 1 else e
-                m.g_p[mem, 1024 + first * HD:1024 + (e + 1) * HD] = side_by_side(blocks[first:])
+                m.g_p[mem, 1024 + first * HD:1024 + (e + 1) * HD] = side_by_side(blocks[2 * first:])
         slope = m.sig[...] * (1.0 - m.sig[...]) * m.hot[...]
         lo_cot = ((m.vg[0] + m.ogc[...]) * slope).astype(BF)
         ln_cot = (m.vg[1] * slope).astype(BF)
@@ -1046,8 +1124,6 @@
         lane = lax.broadcasted_iota(jnp.int32, (SEG, 128), 1)
         m.g_p[mem, 3200:3328] = jnp.where(lane < LOGIT, m.g_p[mem, 3200:3328], both)
         gp_copy().start()
-        ex.tick(7)
-        ex.begin(8)
 
         def norm1_back(rows):
             unit, inv = unit_rows(m.x[rows, :].astype(F32))
@@ -1059,14 +1135,14 @@
         l_ig.start()
         at_copy(2, 1).wait_send()
         turn(4, 1, m.hn[...])
-        ex.tick(8)
+        ex.serve("ln1b")
         gp_copy().wait_recv()
         at_copy(3, 1).wait_recv()
 
-        def proj_grad(i, _):
-            tiles(3, m.g_p[:, two(i)], 82 + 2 * i)
-            return 0
-        lax.fori_loop(0, 12, proj_grad, 0)
+        for i in range(6):
+            tiles(3, m.g_p[:, 4 * TILE * i:4 * TILE * (i + 1)], 82 + 4 * i)
+            if i in (1, 3):
+                ex.serve(f"dwp{i // 2}")
         last = product(3, m.g_p[:, 3072:3328])
         store_tile(parts, 106, last[:, :TILE])
         last = last[:, TILE:]
@@ -1077,10 +1153,8 @@
             last += product(i, jnp.where(lane == at, 1.0, 0.0).astype(BF))
         store_tile(parts, 107, last)
 
-        ex.begin(9)
-        for i in range(9, NS + 5):
-            ex.tick(i)
-            ex.begin(i + 1)
+        ex.serve("dwp2")
+        ex.serve("rest")
         ex.finish()
         l_ig.wait()
 
@@ -1093,7 +1167,8 @@
     @pl.when(t < last_t)
     def _():
         k_copy().wait_send()
-        v_copy().wait_send()
+        v_copy(0).wait_send()
+        v_copy(1).wait_send()
 
     @pl.when(t > 0)
     def _():
@@ -1102,11 +1177,6 @@
 
 
 def tables():
-    col = np.arange(HD)[None, None, :] // DH * E + np.arange(E)[:, None, None]
-    branch = np.arange(128)[None, :, None]
-    exv = branch == LOGIT + col
-    exo = branch == LOGIT + H * E + col
-    exv, exo = (np.concatenate([v, v], axis=1) for v in (exv, exo))
     lane = np.arange(128) - LOGIT
     inside = (lane >= 0) & (lane < 2 * H * E)
     pick = (np.arange(2 * H)[:, None] == lane[None, :] // E) & inside
@@ -1114,13 +1184,13 @@
     spread[:2 * H, :128] = pick
     spread[16:16 + 2 * H, 128:] = pick
     spread[127, :128] = np.where(inside, lane % E, -1)
-    return tuple(v.astype(ml_dtypes.bfloat16) for v in (exv, exo, spread))
+    return spread.astype(ml_dtypes.bfloat16)
 
 
 def fused_device(layer_input, routes, memory_lengths, norm_gains, w_query, w_key, w_value,
                  w_router, w_output, w_up, w_down, output_cot):
     anywhere = pl.BlockSpec(memory_space=pl.ANY)
-    specs = [anywhere] * 15
+    specs = [anywhere] * 13
     specs[2] = pl.BlockSpec(memory_space=pltpu.SMEM)
     out, grad, flat = pl.pallas_call(
         layer_kernel,
@@ -1133,7 +1203,7 @@
             collective_id=0, has_side_effects=True, vmem_limit_bytes=VMEM_LIMIT),
         name="layer",
     )(layer_input[0], jnp.transpose(routes[0], (1, 2, 0)), memory_lengths, norm_gains, w_query.T, w_key.T, w_value.T, w_router.T,
-      w_output, w_up, w_down, output_cot[0], *tables())
+      w_output, w_up, w_down, output_cot[0], tables())
     shapes = ((SEG, D), BF), ((SEG, D), F32), ((2, 32), F32), ((32, HD), F32), ((32, HD), F32), \
         ((32, WIDE), F32), ((32, 2 * H * E), F32), ((32, WIDE), F32), ((32, FF), F32), ((32, FF), F32)
     vm = pl.BlockSpec(memory_space=pltpu.VMEM)

time: 150 us -> 148 us (0.987)
  Pallas kernels: 148 us -> 146 us
    pallas_call x1, Pallas kernels: 145 us -> 143 us  [fused_device(): pl.pallas_call(layer_kernel, out_shape=(jax.ShapeDtypeStruct((SEG, D), BF...]
where the time goes in v3:
time: 148 us
  Pallas kernels  146 us (99%)
  between operations  1.5 us (1%)
    pallas_call x1, Pallas kernels, fused_device(): pl.pallas_call(layer_kernel, out_shape=(jax.ShapeDtypeStruct((SEG, D), BF...  143 us
    pallas_call x1, Pallas kernels, fused_device(): pl.pallas_call(split_kernel, out_shape=tuple((jax.ShapeDtypeStruct(*v) fo...  3.68 us

profile of v3, /device:TPU:0, one launch (start us, length us, event | category | flops | bytes accessed | tf_op | source)
XLA Modules:
  0.0 147.8 jit_solution(4116182171566330673)
XLA Ops:
  1.3 142.6 %layer.1 = (bf16[256,1024]{1,0:T(8,128)(2,1)}, f32[256,1024]{1,0:T(8,128)}, f32[32,13824]{1,0:T(8,128)}) custom-call(bf16[256,1024]{1,0:T(8,128)(2,1)} %bitcast.16, s32[8,2,256]{2,1,0:T(2,128)} %bitcast.19, s32[1,1]{1,0:T(1,128)S(6)} %copy.23.len_s, bf16[2,1024]{1,0:T(2,128)(2,1)} %gains_h.1, bf16[448,1024]{1,0:T(8,128)(2,1)} %bitcast.14, ...), custom_call_target="tpu_custom_call" | custom-call | tf_op jit(solution)/shard_map/layer/pallas_call | solution.py:1195
  143.9 3.7 %split.1 = (bf16[256,1024]{1,0:T(8,128)(2,1)}, f32[256,1024]{1,0:T(8,128)}, f32[2,32]{1,0:T(2,128)}, f32[32,448]{1,0:T(8,128)}, f32[32,448]{1,0:T(8,128)}, /*ind...) custom-call(bf16[256,1024]{1,0:T(8,128)(2,1)} %get-tuple-element.23.out_h, ...), custom_call_target="tpu_custom_call" | custom-call | tf_op jit(solution)/shard_map/split/pallas_call | solution.py:1210

commit v4 on v3

--- a/solution.py
+++ b/solution.py
@@ -254,7 +254,7 @@
 
 MESH_ID = pl.DeviceIdType.MESH
 TILE = 128
-PIECES = [(4, 2), (7, 2), (6, 2), (7, 2), (7, 2), (6, 2), (7, 2), (7, 2), (7, 2), (6, 2), (5, 2), (5, 2), (5, 1), (3, 1)]
+PIECES = [(4, 2)] + [(7, 2)] * 10 + [(6, 2), (3, 1)]
 NS = len(PIECES)
 TILES = sum(a + b for a, b in PIECES)
 FLAT = TILES * TILE
@@ -271,7 +271,7 @@
 POINTS = ([("d0", 4), ("u0", 8), ("j1", 16)] + [(f"j{j}", 8 * j) for j in range(2, 8)] + [("dw7", 64), ("ln2b", 64)]
           + [(f"tho{e}", 64) for e in range(E)] + [("sb0", 64), ("sb1", 64), ("dwo0", 70), ("dwo1", 76), ("dwo2", 82)]
           + [(f"tv{e}", 82) for e in range(E)] + [("ln1b", 82), ("dwp0", 90), ("dwp1", 98), ("dwp2", 108)])
-ROUNDS = ['j2', 'j4', 'j6', 'tho0', 'sb0', 'dwo1', 'tv1', 'tv4', 'dwp1']
+ROUNDS = ["j2", "j4", "j7", "tho1", "sb1", "dwo2", "tv2", "ln1b", "dwp1"]
 
 
 def plan():

time: 148 us -> 148 us (level)
  no operation moved by 1% of the time
where the time goes in v4:
time: 148 us; the launch traced here: 147 us
  Pallas kernels  146 us (99%)
  between operations  1.5 us (1%)
    pallas_call x1, Pallas kernels, fused_device(): pl.pallas_call(layer_kernel, out_shape=(jax.ShapeDtypeStruct((SEG, D), BF...  142 us
    pallas_call x1, Pallas kernels, fused_device(): pl.pallas_call(split_kernel, out_shape=tuple((jax.ShapeDtypeStruct(*v) fo...  3.68 us

profile of v4, /device:TPU:0, one launch (start us, length us, event | category | flops | bytes accessed | tf_op | source)
XLA Modules:
  0.0 147.4 jit_solution(16900825267971180658)
XLA Ops:
  1.3 142.2 %layer.1 = (bf16[256,1024]{1,0:T(8,128)(2,1)}, f32[256,1024]{1,0:T(8,128)}, f32[32,13824]{1,0:T(8,128)}) custom-call(bf16[256,1024]{1,0:T(8,128)(2,1)} %bitcast.16, s32[8,2,256]{2,1,0:T(2,128)} %bitcast.19, s32[1,1]{1,0:T(1,128)S(6)} %copy.23.len_s, bf16[2,1024]{1,0:T(2,128)(2,1)} %gains_h.1, bf16[448,1024]{1,0:T(8,128)(2,1)} %bitcast.14, ...), custom_call_target="tpu_custom_call" | custom-call | tf_op jit(solution)/shard_map/layer/pallas_call | solution.py:1195
  143.5 3.7 %split.1 = (bf16[256,1024]{1,0:T(8,128)(2,1)}, f32[256,1024]{1,0:T(8,128)}, f32[2,32]{1,0:T(2,128)}, f32[32,448]{1,0:T(8,128)}, f32[32,448]{1,0:T(8,128)}, /*ind...) custom-call(bf16[256,1024]{1,0:T(8,128)(2,1)} %get-tuple-element.23.out_h, ...), custom_call_target="tpu_custom_call" | custom-call | tf_op jit(solution)/shard_map/split/pallas_call | solution.py:1210

commit v5 on v4

--- a/solution.py
+++ b/solution.py
@@ -816,19 +816,12 @@
         def norm1(rows):
             unit, _ = unit_rows(m.x[rows, :].astype(F32))
             m.xn[rows, :] = (unit * m.gains[0:1, :].astype(F32)).astype(BF)
-        for_rows(32, norm1)
+        for_rows(64, norm1)
         l_k.wait()
         for half in range(2):
             m.k[half, own] = dot_nt(m.xn[...], m.wk[half_rows(half), :]).astype(BF)
         l_q = load(8, wq_h, m.wq)
         l_oc = load(9, oc_h, m.oc)
-        l_wo = [expert_loads(1, e, e, wo_h, wo.at[pl.ds(e * HD, HD)]) for e in range(E)]
-        for group in l_wo:
-            for cp in group:
-                cp.start()
-        for j in range(2):
-            for cp in ff_loads(j):
-                cp.start()
         pl.semaphore_wait(bar, peers)
 
         @pl.when(t < last_t)
@@ -859,6 +852,14 @@
                         cp.wait()
                 total = total + dot_nt(m.xn[...], wv[e, half_rows(half)]) * gates_wide(m.exv, half, e)
             m.v[half, own] = total.astype(BF)
+            if half == 0:
+                l_wo = [expert_loads(1, e, e, wo_h, wo.at[pl.ds(e * HD, HD)]) for e in range(E)]
+                for group in l_wo:
+                    for cp in group:
+                        cp.start()
+                for j in range(2):
+                    for cp in ff_loads(j):
+                        cp.start()
 
             @pl.when(t < last_t)
             def _():
@@ -909,7 +910,7 @@
         def norm2(rows):
             unit, _ = unit_rows(m.mid[rows, :])
             m.hn[rows, :] = (unit * m.gains[1:2, :].astype(F32)).astype(BF)
-        for_rows(32, norm2)
+        for_rows(64, norm2)
         at_copy(0, 0).wait_send()
         turn(1, 0, m.hn[...])
 

time: 148 us -> 146 us (0.986)
  Pallas kernels: 146 us -> 144 us
where the time goes in v5:
time: 146 us
  Pallas kernels  144 us (99%)
  between operations  1.5 us (1%)
    pallas_call x1, Pallas kernels, fused_device(): pl.pallas_call(layer_kernel, out_shape=(jax.ShapeDtypeStruct((SEG, D), BF...  141 us
    pallas_call x1, Pallas kernels, fused_device(): pl.pallas_call(split_kernel, out_shape=tuple((jax.ShapeDtypeStruct(*v) fo...  3.68 us

profile of v5, /device:TPU:0, one launch (start us, length us, event | category | flops | bytes accessed | tf_op | source)
XLA Modules:
  0.0 145.9 jit_solution(16585087097163146273)
XLA Ops:
  1.3 140.7 %layer.1 = (bf16[256,1024]{1,0:T(8,128)(2,1)}, f32[256,1024]{1,0:T(8,128)}, f32[32,13824]{1,0:T(8,128)}) custom-call(bf16[256,1024]{1,0:T(8,128)(2,1)} %bitcast.16, s32[8,2,256]{2,1,0:T(2,128)} %bitcast.19, s32[1,1]{1,0:T(1,128)S(6)} %copy.23.len_s, bf16[2,1024]{1,0:T(2,128)(2,1)} %gains_h.1, bf16[448,1024]{1,0:T(8,128)(2,1)} %bitcast.14, ...), custom_call_target="tpu_custom_call" | custom-call | tf_op jit(solution)/shard_map/layer/pallas_call | solution.py:1196
  142.0 3.7 %split.1 = (bf16[256,1024]{1,0:T(8,128)(2,1)}, f32[256,1024]{1,0:T(8,128)}, f32[2,32]{1,0:T(2,128)}, f32[32,448]{1,0:T(8,128)}, f32[32,448]{1,0:T(8,128)}, /*ind...) custom-call(bf16[256,1024]{1,0:T(8,128)(2,1)} %get-tuple-element.23.out_h, ...), custom_call_target="tpu_custom_call" | custom-call | tf_op jit(solution)/shard_map/split/pallas_call | solution.py:1211
